TPU v7x, 512 devices: a whole 4x4x16 slice. The times are simulated.
512 devices in a mesh: ctx: 64 (over z, y_lo, core), head: 8 (over y_hi, x).
Axes of the slice: x: 4, y: 4 (y_hi: 2, y_lo: 2; y = y_hi * 2 + y_lo), z: 16, core: 2. Of those that a mesh axis runs over, the one named last changes fastest.
Arguments:
- queries: float32 [16384, 32, 128], P(('ctx', 'head')), may hold values from -6.1 to 6.1
- keys: float32 [16384, 16, 128], P(('ctx', 'head')), may hold values from -6.1 to 6.1
- values: float32 [16384, 16, 128], P(('ctx', 'head')), may hold values from -6 to 6
- out_grad: float32 [16384, 32, 128], P(('ctx', 'head')), may hold values from -6 to 6
Outputs:
- attention: float32 [16384, 32, 128], P(('ctx', 'head'))
- query_grad: float32 [16384, 32, 128], P(('ctx', 'head'))
- key_grad: float32 [16384, 16, 128], P(('ctx', 'head'))
- value_grad: float32 [16384, 16, 128], P(('ctx', 'head'))
All inputs are finite; a program needn't handle non-finite values.
Results may differ from a plain program's by a relative error of at most 0.0003.
Values sent between devices are 32-bit elements; how exact they have to be, the bound alone decides.
No kernel may reach another device: no remote copies, remote signals or barrier semaphores. Data moves between devices by JAX's collectives and lax.ppermute only.
A program may use at most 64 MiB of HBM per device.

v0:
```python
import jax
import jax.numpy as jnp
from jax import lax
from jax.sharding import PartitionSpec as P

WINDOW = 1024


query_scale = 168.0 ** (-0.5)
highest = lax.Precision.HIGHEST


def sent_together(arrays, axis, split_dim, concat_dim, along):
    widths = [a.shape[along] for a in arrays]
    both = jnp.concatenate(arrays, axis=along)
    result = lax.all_to_all(both, axis, split_axis=split_dim, concat_axis=concat_dim, tiled=True)
    return tuple(jnp.split(result, [sum(widths[:k]) for k in range(1, len(widths))], axis=along))


def passed_along(value, axis, steps):
    count = lax.axis_size(axis)
    first, last = (max(0, -steps), min(count, count - steps))
    return lax.ppermute(value, axis, [(source, source + steps) for source in range(first, last)])


def attend(query_rows, grad_rows, key_rows, value_rows, anchor):
    row_count, head_count, head_dim = query_rows.shape
    groups = key_rows.shape[1]
    group_size = head_count // groups
    key_count = key_rows.shape[0]
    grouped = query_rows.reshape(row_count, groups, group_size, head_dim)
    grad_grouped = grad_rows.reshape(row_count, groups, group_size, head_dim)
    scores = jnp.einsum("rgeh,cgh->gerc", grouped, key_rows, precision=highest) * query_scale
    row_iota = lax.broadcasted_iota(jnp.int32, (row_count, key_count), 0)
    col_iota = lax.broadcasted_iota(jnp.int32, (row_count, key_count), 1)
    offset = row_iota - col_iota + WINDOW
    position = anchor - WINDOW + col_iota
    allowed = (offset >= 0) & (offset < WINDOW) & (position >= 0)
    row_max = jnp.max(jnp.where(allowed, scores, -jnp.inf), axis=-1, keepdims=True)
    weights = jnp.exp(jnp.where(allowed, scores - row_max, -jnp.inf))
    normed = weights / jnp.sum(weights, axis=-1, keepdims=True)
    attention = jnp.einsum("gerc,cgh->rgeh", normed, value_rows, precision=highest)
    row_dots = jnp.transpose(jnp.sum(grad_grouped * attention, axis=-1), (1, 2, 0))[..., None]
    prob_grad = jnp.einsum("rgeh,cgh->gerc", grad_grouped, value_rows, precision=highest)
    score_grad = normed * (prob_grad - row_dots)
    query_grad = jnp.einsum("gerc,cgh->rgeh", score_grad, key_rows, precision=highest) * query_scale
    key_grad = jnp.einsum("gerc,rgeh->cgh", score_grad, grouped, precision=highest) * query_scale
    value_grad = jnp.einsum("gerc,rgeh->cgh", normed, grad_grouped, precision=highest)
    shape_out = (row_count, head_count, head_dim)
    return (attention.reshape(shape_out), query_grad.reshape(shape_out), key_grad, value_grad)


def per_device(queries, keys, values, out_grad):
    local_queries, local_grads, local_keys, local_values = (
        *sent_together((queries, out_grad), "head", 1, 0, 2),
        *sent_together((keys, values), "head", 1, 0, 2),
    )
    shard_rows = local_queries.shape[0]
    blocks_back = WINDOW // shard_rows
    anchor = lax.axis_index("ctx") * shard_rows
    keys_values = jnp.stack([local_keys, local_values])
    pieces = []
    for distance in range(blocks_back, 0, -1):
        pieces.append(passed_along(keys_values, "ctx", distance))
    border = jnp.concatenate(pieces, axis=1)
    window_rows = jnp.concatenate([border, keys_values], axis=1)
    attention, query_grad, key_grad, value_grad = attend(
        local_queries, local_grads, window_rows[0], window_rows[1], anchor
    )
    gradients = jnp.stack([key_grad, value_grad])
    local_part = gradients[:, WINDOW:]
    totals = local_part
    for distance in range(1, blocks_back + 1):
        offset_at = WINDOW - distance * shard_rows
        totals = totals + passed_along(
            gradients[:, offset_at : offset_at + shard_rows], "ctx", -distance
        )
    return (
        *sent_together((attention, query_grad), "head", 0, 1, 2),
        *sent_together((totals[0], totals[1]), "head", 0, 1, 2),
    )


def solution(mesh):
    placed = (
        P(("ctx", "head"), None, None),
        P(("ctx", "head"), None, None),
        P(("ctx", "head"), None, None),
        P(("ctx", "head"), None, None),
    )
    return jax.shard_map(
        per_device,
        mesh=mesh,
        in_specs=placed,
        out_specs=(
            P(("ctx", "head"), None, None),
            P(("ctx", "head"), None, None),
            P(("ctx", "head"), None, None),
            P(("ctx", "head"), None, None),
        ),
        check_vma=False,
    )
```

profile of v0, /device:TPU:384, one launch (start us, length us, event | category | flops | bytes accessed | tf_op | source)
XLA Modules:
  0.0 171.8 jit_solution(2043666947939062659)
XLA Ops:
  3.6 6.9 %all-to-all-start = ((f32[32,16,256]{2,0,1:T(8,128)}), f32[32,16,256]{2,0,1:T(8,128)S(1)}, u32[]{:S(2)}, u32[]{:S(2)}) async-start(f32[32,16,256]{2,0,1:T(8,128)} %pad_maximum_fusion.3), calls=%async_computation | async-start | bytes 1048576 | tf_op jit(solution)/shard_map/all_to_all | solution.py:16
  12.3 9.9 %all-to-all-done = f32[32,16,256]{2,0,1:T(8,128)S(1)} async-done(((f32[32,16,256]{2,0,1:T(8,128)}), f32[32,16,256]{2,0,1:T(8,128)S(1)}, u32[]{:S(2)}, u32[]{:S(2)}) %all-to-all-start) | async-done | bytes 524320 | tf_op jit(solution)/shard_map/all_to_all | solution.py:16
  22.2 3.6 %all-to-all-start.1 = ((f32[32,32,256]{2,0,1:T(8,128)}), f32[32,32,256]{2,0,1:T(8,128)S(1)}, u32[]{:S(2)}, u32[]{:S(2)}) async-start(f32[32,32,256]{2,0,1:T(8,128)} %pad_maximum_fusion), calls=%async_computation.1 | async-start | bytes 2097152 | tf_op jit(solution)/shard_map/all_to_all | solution.py:16
  25.9 2.9 %collective-permute-start = (f32[2,256,2,128]{3,1,2,0:T(8,128)S(1)}, f32[2,256,2,128]{3,1,2,0:T(8,128)}, u32[]{:S(2)}, u32[]{:S(2)}) collective-permute-start(f32[2,256,2,128]{3,1,2,0:T(8,128)S(1)} %pad_maximum_fusion.4), channel_id=1, source_target_pairs={{0,32},{8,40},{16,48},{24,56},{32,64},{40,72},{48,80},{56,88},{64,... | collective-permute-start | bytes 1572872 | tf_op jit(solution)/shard_map/ppermute | solution.py:23
  30.7 3.4 %collective-permute-start.2 = (f32[2,256,2,128]{3,1,2,0:T(8,128)S(1)}, f32[2,256,2,128]{3,1,2,0:T(8,128)}, u32[]{:S(2)}, u32[]{:S(2)}) collective-permute-start(f32[2,256,2,128]{3,1,2,0:T(8,128)S(1)} %pad_maximum_fusion.4), channel_id=1, source_target_pairs={{0,16},{8,24},{16,32},{24,40},{32,48},{40,56},{48,64},{56,72},{64,... | collective-permute-start | bytes 1572872 | tf_op jit(solution)/shard_map/ppermute | solution.py:23
  36.3 6.7 %all-to-all-done.1 = f32[32,32,256]{2,0,1:T(8,128)S(1)} async-done(((f32[32,32,256]{2,0,1:T(8,128)}), f32[32,32,256]{2,0,1:T(8,128)S(1)}, u32[]{:S(2)}, u32[]{:S(2)}) %all-to-all-start.1) | async-done | bytes 1048608 | tf_op jit(solution)/shard_map/all_to_all | solution.py:16
  45.0 3.9 %collective-permute-done.1 = f32[2,256,2,128]{3,1,2,0:T(8,128)} collective-permute-done((f32[2,256,2,128]{3,1,2,0:T(8,128)S(1)}, f32[2,256,2,128]{3,1,2,0:T(8,128)}, u32[]{:S(2)}, u32[]{:S(2)}) %collective-permute-start.1) | collective-permute-done | bytes 524320 | tf_op jit(solution)/shard_map/ppermute | solution.py:23
  50.0 16.5 %collective-permute-done.2 = f32[2,256,2,128]{3,1,2,0:T(8,128)} collective-permute-done((f32[2,256,2,128]{3,1,2,0:T(8,128)S(1)}, f32[2,256,2,128]{3,1,2,0:T(8,128)}, u32[]{:S(2)}, u32[]{:S(2)}) %collective-permute-start.2) | collective-permute-done | bytes 524320 | tf_op jit(solution)/shard_map/ppermute | solution.py:23
  67.6 3.2 %collective-permute-done.3 = f32[2,256,2,128]{3,1,2,0:T(8,128)} collective-permute-done((f32[2,256,2,128]{3,1,2,0:T(8,128)S(1)}, f32[2,256,2,128]{3,1,2,0:T(8,128)}, u32[]{:S(2)}, u32[]{:S(2)}) %collective-permute-start.3) | collective-permute-done | bytes 524320 | tf_op jit(solution)/shard_map/ppermute | solution.py:23
  71.9 4.4 %fusion.16 = f32[2,1280,256,2]{2,1,3,0:T(8,128)S(1)} fusion(f32[256,2,2,128]{3,0,2,1:T(8,128)S(1)} %bitcast.104, f32[2,1280,2,128]{3,1,2,0:T(8,128)S(1)} %constant_dynamic-update-slice_fusion), kind=kOutput, calls=%fused_computation.34 | convolution fusion | flops 2013265920 | bytes 7077888 | tf_op jit(solution)/shard_map/rgeh,cgh->gerc/dot_general | solution.py:33
  76.3 2.9 %fusion.31 = (f32[2,2,256]{2,1,0:T(2,128)S(1)}, f32[2,2,256,1280]{2,3,1,0:T(8,128)S(1)}) fusion(f32[2,1280,256,2]{2,1,3,0:T(8,128)S(1)} %fusion.16, pred[256,1280]{0,1:T(8,128)(4,1)S(1)} %fusion.14), kind=kOutput, calls=%fused_computation.66 | output fusion | flops 7865599 | bytes 10817536 | tf_op jit(solution)/shard_map/sub | solution.py:40
  79.2 4.4 %fusion.25 = (f32[256,2,2]{0,2,1:T(2,128)S(1)}, f32[2,128,2,256]{3,1,2,0:T(8,128)}) fusion(f32[256,2,2,128]{0,3,2,1:T(8,128)S(1)} %bitcast.117, f32[2,2,256,1280]{2,3,1,0:T(8,128)S(1)} %get-tuple-element.27, f32[2,2,256]{2,1,0:T(2,128)S(1)} %get-tuple-element.26, f32[2,1280,2,128]{3,1,2,0:T(8,128)S(1)} %constant_dynamic-update-slice_fusion), kind=kOutput, calls=%fused_computation.50 | convolution fusion | flops 2014837760 | bytes 7610368 | tf_op jit(solution)/shard_map/gerc,cgh->rgeh/dot_general | solution.py:42
  83.6 5.7 %convolution_bitcast_fusion = f32[1,1280,2,128]{1,3,2,0:T(8,128)S(1)} fusion(f32[256,2,2,128]{3,0,2,1:T(8,128)S(1)} %bitcast.115, f32[2,2,256,1280]{2,3,1,0:T(8,128)S(1)} %get-tuple-element.27, f32[2,2,256]{2,1,0:T(2,128)S(1)} %get-tuple-element.26), kind=kOutput, calls=%fused_computation.17 | convolution fusion | flops 2014576640 | bytes 7081984 | tf_op jit(solution)/shard_map/gerc,rgeh->cgh/dot_general | solution.py:48
  89.3 5.1 %fusion.1 = f32[2,2,256,1280]{2,3,1,0:T(8,128)S(1)} fusion(f32[256,2,2,128]{3,0,2,1:T(8,128)S(1)} %bitcast.116, f32[2,2,256]{2,1,0:T(2,128)S(1)} %bitcast.119, f32[2,1280,2,128]{3,1,2,0:T(8,128)S(1)} %constant_dynamic-update-slice_fusion, f32[2,2,256,1280]{2,3,1,0:T(8,128)S(1)} %get-tuple-element.27, f32[2,2,256]{2,1,0:T(2,128)S(1)} %get-tuple-element.26), kind=kOutput, calls=%fused_computation.2 | convolution fusion | flops 2017198080 | bytes 12328960 | tf_op jit(solution)/shard_map/rgeh,cgh->gerc/dot_general | solution.py:44
  94.4 5.6 %fusion.7 = f32[1,1280,2,128]{1,3,2,0:T(8,128)S(1)} fusion(f32[256,2,2,128]{3,0,2,1:T(8,128)S(1)} %bitcast.105, f32[2,2,256,1280]{2,3,1,0:T(8,128)S(1)} %fusion.1), kind=kOutput, calls=%fused_computation.20 | convolution fusion | flops 2013593600 | bytes 7077888 | tf_op jit(solution)/shard_map/gerc,rgeh->cgh/dot_general | solution.py:47
  101.4 2.9 %collective-permute-start.7 = (f32[2,256,2,128]{1,3,2,0:T(8,128)}, f32[2,256,2,128]{1,3,2,0:T(8,128)}, u32[]{:S(2)}, u32[]{:S(2)}) collective-permute-start(f32[2,256,2,128]{1,3,2,0:T(8,128)} %get-tuple-element.14), channel_id=1, source_target_pairs={{32,0},{40,8},{48,16},{56,24},{64,32},{72,40},{80,48},{88,56},{96,... | collective-permute-start | bytes 1572872 | tf_op jit(solution)/shard_map/ppermute | solution.py:23
  108.1 4.1 %collective-permute-start.4 = (f32[2,256,2,128]{1,3,2,0:T(8,128)}, f32[2,256,2,128]{1,3,2,0:T(8,128)}, u32[]{:S(2)}, u32[]{:S(2)}) collective-permute-start(f32[2,256,2,128]{1,3,2,0:T(8,128)} %get-tuple-element.12), channel_id=1, source_target_pairs={{8,0},{16,8},{24,16},{32,24},{40,32},{48,40},{56,48},{64,56},{72,6... | collective-permute-start | bytes 1572872 | tf_op jit(solution)/shard_map/ppermute | solution.py:23
  112.2 3.5 %convolution_multiply_fusion = f32[2,128,2,256]{3,1,2,0:T(8,128)S(1)} fusion(f32[2,2,256,1280]{2,3,1,0:T(8,128)S(1)} %fusion.1, f32[2,1280,2,128]{3,1,2,0:T(8,128)S(1)} %constant_dynamic-update-slice_fusion), kind=kOutput, calls=%fused_computation.32 | convolution fusion | flops 2013396992 | bytes 7077888 | tf_op jit(solution)/shard_map/gerc,cgh->rgeh/dot_general | solution.py:46
  120.3 7.5 %all-to-all-start.2 = ((f32[256,4,256]{2,1,0:T(4,128)}), f32[256,4,256]{2,1,0:T(4,128)}, u32[]{:S(2)}, u32[]{:S(2)}) async-start(f32[256,4,256]{2,1,0:T(4,128)} %pad_maximum_fusion.1), calls=%async_computation.2 | async-start | bytes 2097152 | tf_op jit(solution)/shard_map/all_to_all | solution.py:16
  127.7 5.5 %collective-permute-done.5 = f32[2,256,2,128]{1,3,2,0:T(8,128)} collective-permute-done((f32[2,256,2,128]{1,3,2,0:T(8,128)}, f32[2,256,2,128]{1,3,2,0:T(8,128)}, u32[]{:S(2)}, u32[]{:S(2)}) %collective-permute-start.5) | collective-permute-done | bytes 524320 | tf_op jit(solution)/shard_map/ppermute | solution.py:23
  133.2 12.6 %collective-permute-done.4 = f32[2,256,2,128]{1,3,2,0:T(8,128)} collective-permute-done((f32[2,256,2,128]{1,3,2,0:T(8,128)}, f32[2,256,2,128]{1,3,2,0:T(8,128)}, u32[]{:S(2)}, u32[]{:S(2)}) %collective-permute-start.4) | collective-permute-done | bytes 524320 | tf_op jit(solution)/shard_map/ppermute | solution.py:23
  148.7 5.2 %all-to-all-done.2 = f32[256,4,256]{2,1,0:T(4,128)} async-done(((f32[256,4,256]{2,1,0:T(4,128)}), f32[256,4,256]{2,1,0:T(4,128)}, u32[]{:S(2)}, u32[]{:S(2)}) %all-to-all-start.2) | async-done | bytes 1048608 | tf_op jit(solution)/shard_map/all_to_all | solution.py:16
  153.8 4.3 %all-to-all-start.3 = ((f32[256,2,256]{2,1,0:T(2,128)}), f32[256,2,256]{2,1,0:T(2,128)S(1)}, u32[]{:S(2)}, u32[]{:S(2)}) async-start(f32[256,2,256]{2,1,0:T(2,128)} %copy.74), calls=%async_computation.3 | async-start | bytes 1048576 | tf_op jit(solution)/shard_map/all_to_all | solution.py:16
  162.0 7.9 %all-to-all-done.3 = f32[256,2,256]{2,1,0:T(2,128)S(1)} async-done(((f32[256,2,256]{2,1,0:T(2,128)}), f32[256,2,256]{2,1,0:T(2,128)S(1)}, u32[]{:S(2)}, u32[]{:S(2)}) %all-to-all-start.3) | async-done | bytes 524320 | tf_op jit(solution)/shard_map/all_to_all | solution.py:16
  (48 shorter events, 32.3 us)
Async XLA Ops:
  0.6 9.9 %copy-start = (f32[32,32,128]{2,1,0:T(8,128)S(1)}, f32[32,32,128]{2,1,0:T(8,128)}, u32[]{:S(2)}) copy-start(f32[32,32,128]{2,1,0:T(8,128)} %param.7) | copy-start | bytes 1572868
  0.6 10.3 %copy-start.1 = (f32[32,32,128]{2,1,0:T(8,128)S(1)}, f32[32,32,128]{2,1,0:T(8,128)}, u32[]{:S(2)}) copy-start(f32[32,32,128]{2,1,0:T(8,128)} %param.4) | copy-start | bytes 1572868
  3.6 18.5 %all-to-all-start = ((f32[32,16,256]{2,0,1:T(8,128)}), f32[32,16,256]{2,0,1:T(8,128)S(1)}, u32[]{:S(2)}, u32[]{:S(2)}) async-start(f32[32,16,256]{2,0,1:T(8,128)} %pad_maximum_fusion.3), calls=%async_computation | async-start | bytes 1048576 | tf_op jit(solution)/shard_map/all_to_all | solution.py:16
  22.2 20.9 %all-to-all-start.1 = ((f32[32,32,256]{2,0,1:T(8,128)}), f32[32,32,256]{2,0,1:T(8,128)S(1)}, u32[]{:S(2)}, u32[]{:S(2)}) async-start(f32[32,32,256]{2,0,1:T(8,128)} %pad_maximum_fusion), calls=%async_computation.1 | async-start | bytes 2097152 | tf_op jit(solution)/shard_map/all_to_all | solution.py:16
  25.9 18.0 %collective-permute-start = (f32[2,256,2,128]{3,1,2,0:T(8,128)S(1)}, f32[2,256,2,128]{3,1,2,0:T(8,128)}, u32[]{:S(2)}, u32[]{:S(2)}) collective-permute-start(f32[2,256,2,128]{3,1,2,0:T(8,128)S(1)} %pad_maximum_fusion.4), channel_id=1, source_target_pairs={{0,32},{8,40},{16,48},{24,56},{32,64},{40,72},{48,80},{56,88},{64,... | collective-permute-start | bytes 1572872 | tf_op jit(solution)/shard_map/ppermute | solution.py:23
  28.8 20.1 %collective-permute-start.1 = (f32[2,256,2,128]{3,1,2,0:T(8,128)S(1)}, f32[2,256,2,128]{3,1,2,0:T(8,128)}, u32[]{:S(2)}, u32[]{:S(2)}) collective-permute-start(f32[2,256,2,128]{3,1,2,0:T(8,128)S(1)} %pad_maximum_fusion.4), channel_id=1, source_target_pairs={{0,24},{8,32},{16,40},{24,48},{32,56},{40,64},{48,72},{56,80},{64,... | collective-permute-start | bytes 1572872 | tf_op jit(solution)/shard_map/ppermute | solution.py:23
  30.7 35.8 %collective-permute-start.2 = (f32[2,256,2,128]{3,1,2,0:T(8,128)S(1)}, f32[2,256,2,128]{3,1,2,0:T(8,128)}, u32[]{:S(2)}, u32[]{:S(2)}) collective-permute-start(f32[2,256,2,128]{3,1,2,0:T(8,128)S(1)} %pad_maximum_fusion.4), channel_id=1, source_target_pairs={{0,16},{8,24},{16,32},{24,40},{32,48},{40,56},{48,64},{56,72},{64,... | collective-permute-start | bytes 1572872 | tf_op jit(solution)/shard_map/ppermute | solution.py:23
  34.4 36.4 %collective-permute-start.3 = (f32[2,256,2,128]{3,1,2,0:T(8,128)S(1)}, f32[2,256,2,128]{3,1,2,0:T(8,128)}, u32[]{:S(2)}, u32[]{:S(2)}) collective-permute-start(f32[2,256,2,128]{3,1,2,0:T(8,128)S(1)} %pad_maximum_fusion.4), channel_id=1, source_target_pairs={{0,8},{8,16},{16,24},{24,32},{32,40},{40,48},{48,56},{56,64},{64,7... | collective-permute-start | bytes 1572872 | tf_op jit(solution)/shard_map/ppermute | solution.py:23
  101.4 26.4 %collective-permute-start.7 = (f32[2,256,2,128]{1,3,2,0:T(8,128)}, f32[2,256,2,128]{1,3,2,0:T(8,128)}, u32[]{:S(2)}, u32[]{:S(2)}) collective-permute-start(f32[2,256,2,128]{1,3,2,0:T(8,128)} %get-tuple-element.14), channel_id=1, source_target_pairs={{32,0},{40,8},{48,16},{56,24},{64,32},{72,40},{80,48},{88,56},{96,... | collective-permute-start | bytes 1572872 | tf_op jit(solution)/shard_map/ppermute | solution.py:23
  104.3 23.5 %collective-permute-start.6 = (f32[2,256,2,128]{1,3,2,0:T(8,128)}, f32[2,256,2,128]{1,3,2,0:T(8,128)}, u32[]{:S(2)}, u32[]{:S(2)}) collective-permute-start(f32[2,256,2,128]{1,3,2,0:T(8,128)} %get-tuple-element.15), channel_id=1, source_target_pairs={{24,0},{32,8},{40,16},{48,24},{56,32},{64,40},{72,48},{80,56},{88,... | collective-permute-start | bytes 1572872 | tf_op jit(solution)/shard_map/ppermute | solution.py:23
  106.2 27.0 %collective-permute-start.5 = (f32[2,256,2,128]{1,3,2,0:T(8,128)}, f32[2,256,2,128]{1,3,2,0:T(8,128)}, u32[]{:S(2)}, u32[]{:S(2)}) collective-permute-start(f32[2,256,2,128]{1,3,2,0:T(8,128)} %get-tuple-element.13), channel_id=1, source_target_pairs={{16,0},{24,8},{32,16},{40,24},{48,32},{56,40},{64,48},{72,56},{80,... | collective-permute-start | bytes 1572872 | tf_op jit(solution)/shard_map/ppermute | solution.py:23
  108.1 37.7 %collective-permute-start.4 = (f32[2,256,2,128]{1,3,2,0:T(8,128)}, f32[2,256,2,128]{1,3,2,0:T(8,128)}, u32[]{:S(2)}, u32[]{:S(2)}) collective-permute-start(f32[2,256,2,128]{1,3,2,0:T(8,128)} %get-tuple-element.12), channel_id=1, source_target_pairs={{8,0},{16,8},{24,16},{32,24},{40,32},{48,40},{56,48},{64,56},{72,6... | collective-permute-start | bytes 1572872 | tf_op jit(solution)/shard_map/ppermute | solution.py:23
  120.3 33.6 %all-to-all-start.2 = ((f32[256,4,256]{2,1,0:T(4,128)}), f32[256,4,256]{2,1,0:T(4,128)}, u32[]{:S(2)}, u32[]{:S(2)}) async-start(f32[256,4,256]{2,1,0:T(4,128)} %pad_maximum_fusion.1), calls=%async_computation.2 | async-start | bytes 2097152 | tf_op jit(solution)/shard_map/all_to_all | solution.py:16
  153.8 16.0 %all-to-all-start.3 = ((f32[256,2,256]{2,1,0:T(2,128)}), f32[256,2,256]{2,1,0:T(2,128)S(1)}, u32[]{:S(2)}, u32[]{:S(2)}) async-start(f32[256,2,256]{2,1,0:T(2,128)} %copy.74), calls=%async_computation.3 | async-start | bytes 1048576 | tf_op jit(solution)/shard_map/all_to_all | solution.py:16
where the time goes:
time: 173 us; the launch traced here: 172 us
  waiting for transfers between devices  71.9 us (42%)
  starting transfers between devices  43.2 us (25%)
  matrix products  28.6 us (17%)
  local copies, waits for them, and re-layouts  16.5 us (10%)
  other arithmetic  10.5 us (6%)
    ppermute x8, waiting for transfers between devices, passed_along(): lax.ppermute(value, axis, [(source, source + steps) for source in range(f...  42.2 us
    all_to_all x4, waiting for transfers between devices, sent_together(): lax.all_to_all(both, axis, split_axis=split_dim, concat_axis=concat_dim,...  29.7 us
    all_to_all x4, starting transfers between devices, sent_together(): lax.all_to_all(both, axis, split_axis=split_dim, concat_axis=concat_dim,...  22.2 us
    ppermute x8, starting transfers between devices, passed_along(): lax.ppermute(value, axis, [(source, source + steps) for source in range(f...  21 us
    unnamed x16, local copies, waits for them, and re-layouts  11 us
    dot_general x1, matrix products, attend(): jnp.einsum('gerc,rgeh->cgh', normed, grad_grouped, precision=highest)  5.7 us
    dot_general x1, matrix products, attend(): jnp.einsum('gerc,rgeh->cgh', score_grad, grouped, precision=highest)  5.58 us
    dot_general x1, matrix products, attend(): jnp.einsum('rgeh,cgh->gerc', grad_grouped, value_rows, precision=highest)  5.06 us
  transfers between devices with their start and end apart: 12, of which 10 were waited for; matrix products, arithmetic and copies ran while one was open for 12% of the time, Pallas kernels for 0%

commit v1 on v0

v1 whole, which is shorter than its diff:
```python
import jax
import jax.numpy as jnp
from jax import lax
from jax.experimental import pallas as pl
from jax.experimental.pallas import tpu as pltpu
from jax.sharding import Mesh, PartitionSpec as P

WINDOW = 1024
HEADS = 32
GROUPS = 16
HEAD_DIM = 128
ROWS = 32
BLOCK = 256
PEERS = 16
PLANE_AXES = ("ylo", "head")

query_scale = 168.0 ** (-0.5)
f32 = jnp.float32
bf16 = jnp.bfloat16

VMEM = pl.BlockSpec(memory_space=pltpu.VMEM)


def params():
    return pltpu.CompilerParams(vmem_limit_bytes=40 * 1024 * 1024)


def pack_kv_kernel(k_ref, v_ref, out_ref):
    for g in range(GROUPS):
        out_ref[g, 0] = k_ref[:, g, :]
        out_ref[g, 1] = v_ref[:, g, :]


def pack_q_kernel(q_ref, d_ref, out_ref):
    for g in range(GROUPS):
        for h in range(2):
            out_ref[g, h] = q_ref[:, 2 * g + h, :]
            out_ref[g, 2 + h] = d_ref[:, 2 * g + h, :]


def unpack_kv_kernel(in_ref, k_ref, v_ref):
    for g in range(GROUPS):
        k_ref[:, g, :] = in_ref[g, 0]
        v_ref[:, g, :] = in_ref[g, 1]


def unpack_q_kernel(in_ref, a_ref, q_ref):
    for g in range(GROUPS):
        for h in range(2):
            a_ref[:, 2 * g + h, :] = in_ref[g, h]
            q_ref[:, 2 * g + h, :] = in_ref[g, 2 + h]


def split(x):
    hi = x.astype(bf16)
    lo = (x - hi.astype(f32)).astype(bf16)
    return hi, lo


def dot(a, b):
    return lax.dot_general(a, b, (((1,), (0,)), ((), ())), preferred_element_type=f32)


def attend_kernel(
    q_ref, own_ref, ownx_ref, halo_ref, halox_ref,
    out_ref, gown_ref, gownx_ref, ghalo_ref, ghalox_ref,
    kcat, vcat, kt, vt, s_ref, w_hi, w_lo, dk, dv,
):
    z = lax.axis_index("z")
    core = lax.axis_index("core")
    other = 1 - core
    for base, mine, ref in ((0, core, halo_ref), (0, other, halox_ref), (4, core, own_ref), (4, other, ownx_ref)):
        for y in range(2):
            at = base + 2 * y + mine
            rows = pl.ds(pl.multiple_of(at * BLOCK, BLOCK), BLOCK)
            for i, cat, tr in ((0, kcat, kt), (1, vcat, vt)):
                x = ref[8 * y : 8 * y + 8, i].reshape(BLOCK, HEAD_DIM)
                hi, lo = split(x)
                cat[rows, :HEAD_DIM] = hi
                cat[rows, HEAD_DIM:] = lo
                thi, tlo = split(x.T)
                tr[at, :HEAD_DIM, :] = thi
                tr[at, HEAD_DIM:, :] = tlo
    dk[...] = jnp.zeros_like(dk)
    dv[...] = jnp.zeros_like(dv)
    key_iota = lax.broadcasted_iota(jnp.int32, (BLOCK, BLOCK), 0)
    query_iota = lax.broadcasted_iota(jnp.int32, (BLOCK, BLOCK), 1)
    for y in range(2):
        first = 2 * y + core
        for h in range(2):
            q = q_ref[8 * y : 8 * y + 8, h].reshape(BLOCK, HEAD_DIM) * query_scale
            d = q_ref[8 * y : 8 * y + 8, 2 + h].reshape(BLOCK, HEAD_DIM)
            q_hi, q_lo = split(q)
            qcat = jnp.concatenate([q_hi, q_lo], axis=1)
            qt_hi, qt_lo = split(q.T)
            qt2 = jnp.concatenate([qt_hi, qt_hi], axis=0)
            dt = d.T
            maxes = []
            for b in range(5):
                rows = pl.ds(pl.multiple_of((first + b) * BLOCK, BLOCK), BLOCK)
                s = dot(kcat[rows, :], qt2) + dot(kcat[rows, :HEAD_DIM], qt_lo)
                if b == 0:
                    s = jnp.where(key_iota > query_iota, s, -jnp.inf)
                if b == 4:
                    s = jnp.where(key_iota <= query_iota, s, -jnp.inf)
                s_ref[b] = s
                m = jnp.max(s, axis=0, keepdims=True)
                exists = (z * 4 + first + b - 4) >= 0
                maxes.append(jnp.where(exists, m, -jnp.inf))
            row_max = maxes[4]
            for b in range(4):
                row_max = jnp.maximum(row_max, maxes[b])
            total = jnp.zeros((1, BLOCK), f32)
            at_sum = jnp.zeros((HEAD_DIM, BLOCK), f32)
            for b in range(5):
                exists = (z * 4 + first + b - 4) >= 0
                shift = jnp.where(exists, row_max, jnp.inf)
                w = jnp.exp(s_ref[b] - shift)
                total = total + jnp.sum(w, axis=0, keepdims=True)
                hi, lo = split(w)
                s_ref[b] = w
                w_hi[b] = hi
                w_lo[b] = lo
                vtb = vt[first + b]
                both = dot(vtb, hi)
                at_sum = at_sum + (both[:HEAD_DIM] + both[HEAD_DIM:] + dot(vtb[:HEAD_DIM], lo))
            inverse = 1.0 / total
            at_sum = at_sum * inverse
            out_ref[8 * y : 8 * y + 8, h] = at_sum.T.reshape(8, ROWS, HEAD_DIM)
            dt = dt * inverse
            row_dots = jnp.sum(dt * at_sum, axis=0, keepdims=True)
            dt_hi, dt_lo = split(dt)
            dt2 = jnp.concatenate([dt_hi, dt_hi], axis=0)
            d_hi, d_lo = split(dt.T)
            dcat = jnp.concatenate([d_hi, d_lo], axis=1)
            dq_sum = jnp.zeros((HEAD_DIM, BLOCK), f32)
            for b in range(5):
                rows = pl.ds(pl.multiple_of((first + b) * BLOCK, BLOCK), BLOCK)
                both = dot(w_hi[b], dcat)
                dv[rows, :] += both[:, :HEAD_DIM] + both[:, HEAD_DIM:] + dot(w_lo[b], d_hi)
                dp = dot(vcat[rows, :], dt2) + dot(vcat[rows, :HEAD_DIM], dt_lo)
                hi, lo = split(s_ref[b] * (dp - row_dots))
                ktb = kt[first + b]
                both = dot(ktb, hi)
                dq_sum = dq_sum + (both[:HEAD_DIM] + both[HEAD_DIM:] + dot(ktb[:HEAD_DIM], lo))
                both = dot(hi, qcat)
                dk[rows, :] += both[:, :HEAD_DIM] + both[:, HEAD_DIM:] + dot(lo, q_hi)
            dq_sum = dq_sum * query_scale
            out_ref[8 * y : 8 * y + 8, 2 + h] = dq_sum.T.reshape(8, ROWS, HEAD_DIM)
    for base, mine, ref in ((0, core, ghalo_ref), (0, other, ghalox_ref), (4, core, gown_ref), (4, other, gownx_ref)):
        for y in range(2):
            rows = pl.ds(pl.multiple_of((base + 2 * y + mine) * BLOCK, BLOCK), BLOCK)
            ref[8 * y : 8 * y + 8, 0] = dk[rows, :].reshape(8, ROWS, HEAD_DIM)
            ref[8 * y : 8 * y + 8, 1] = dv[rows, :].reshape(8, ROWS, HEAD_DIM)


def shape(*dims):
    return jax.ShapeDtypeStruct(dims, f32)


def call(kernel, outs, ins, scratch=()):
    return pl.pallas_call(
        kernel,
        out_shape=outs,
        in_specs=[VMEM] * len(ins),
        out_specs=[VMEM] * len(outs) if isinstance(outs, tuple) else VMEM,
        scratch_shapes=list(scratch),
        compiler_params=params(),
    )(*ins)


def exchanged(x):
    return lax.all_to_all(x, PLANE_AXES, 0, 0, tiled=True)


def swapped(x):
    return lax.ppermute(x, "core", [(0, 1), (1, 0)])


def per_device(queries, keys, values, out_grad):
    planes = lax.axis_size("z")
    kv_shape = shape(PEERS, 2, ROWS, HEAD_DIM)
    q_shape = shape(PEERS, 4, ROWS, HEAD_DIM)
    own = exchanged(call(pack_kv_kernel, kv_shape, (keys, values)))
    rows = exchanged(call(pack_q_kernel, q_shape, (queries, out_grad)))
    halo = lax.ppermute(own, "z", [(i, i + 1) for i in range(planes - 1)])
    ownx = swapped(own)
    halox = swapped(halo)
    scratch = (
        pltpu.VMEM((8 * BLOCK, 2 * HEAD_DIM), bf16),
        pltpu.VMEM((8 * BLOCK, 2 * HEAD_DIM), bf16),
        pltpu.VMEM((8, 2 * HEAD_DIM, BLOCK), bf16),
        pltpu.VMEM((8, 2 * HEAD_DIM, BLOCK), bf16),
        pltpu.VMEM((5, BLOCK, BLOCK), f32),
        pltpu.VMEM((5, BLOCK, BLOCK), bf16),
        pltpu.VMEM((5, BLOCK, BLOCK), bf16),
        pltpu.VMEM((8 * BLOCK, HEAD_DIM), f32),
        pltpu.VMEM((8 * BLOCK, HEAD_DIM), f32),
    )
    out, gown, gownx, ghalo, ghalox = call(
        attend_kernel, (q_shape, kv_shape, kv_shape, kv_shape, kv_shape), (rows, own, ownx, halo, halox), scratch
    )
    back = exchanged(out)
    ghalo = ghalo + swapped(ghalox)
    returned = lax.ppermute(ghalo, "z", [(i + 1, i) for i in range(planes - 1)])
    total = gown + swapped(gownx) + returned
    kv_back = exchanged(total)
    attention, query_grad = call(unpack_q_kernel, (shape(ROWS, HEADS, HEAD_DIM),) * 2, (back,))
    key_grad, value_grad = call(unpack_kv_kernel, (shape(ROWS, GROUPS, HEAD_DIM),) * 2, (kv_back,))
    return attention, query_grad, key_grad, value_grad


def solution(mesh):
    inner = Mesh(mesh.devices.reshape(-1, 2, 2, mesh.shape["head"]), ("z", "ylo", "core", "head"))
    spec = P(("z", "ylo", "core", "head"), None, None)
    return jax.shard_map(per_device, mesh=inner, in_specs=(spec,) * 4, out_specs=(spec,) * 4, check_vma=False)
```

time: 173 us -> 113 us (0.65)
  the two profiles are of different devices: /device:TPU:384 before, /device:TPU:224 now
where the time goes in v1:
time: 113 us
  waiting for transfers between devices  36.6 us (32%)
  starting transfers between devices  29.7 us (26%)
  Pallas kernels  19.5 us (17%)
  blocking collectives  18.5 us (16%)
  local copies, waits for them, and re-layouts  6.37 us (6%)
    pallas_call x5, Pallas kernels, call(): pl.pallas_call(kernel, out_shape=outs, in_specs=[VMEM] * len(ins), out_sp...  19.5 us
    all_to_all x3, waiting for transfers between devices, exchanged(): return lax.all_to_all(x, PLANE_AXES, 0, 0, tiled=True)  18.9 us
    all_to_all x1, blocking collectives, exchanged(): return lax.all_to_all(x, PLANE_AXES, 0, 0, tiled=True)  18.5 us
    ppermute x1, waiting for transfers between devices, per_device(): returned = lax.ppermute(ghalo, 'z', [(i + 1, i) for i in range(planes - 1)])  15 us
    all_to_all x3, starting transfers between devices, exchanged(): return lax.all_to_all(x, PLANE_AXES, 0, 0, tiled=True)  14.6 us
    ppermute x4, starting transfers between devices, swapped(): return lax.ppermute(x, 'core', [(0, 1), (1, 0)])  8.14 us
    unnamed x20, local copies, waits for them, and re-layouts  6.37 us
    ppermute x1, starting transfers between devices, per_device(): halo = lax.ppermute(own, 'z', [(i, i + 1) for i in range(planes - 1)])  5.02 us
  transfers between devices with their start and end apart: 9, of which 4 were waited for; matrix products, arithmetic and copies ran while one was open for 1% of the time, Pallas kernels for 3%

profile of v1, /device:TPU:224, one launch (start us, length us, event | category | flops | bytes accessed | tf_op | source)
XLA Modules:
  0.0 112.5 jit_solution(2372122769520109823)
XLA Ops:
  0.6 0.9 copy-done.6
  1.6 0.9 copy-done.7
  2.8 18.5 %all_to_all.20.own_ref = f32[16,2,32,128]{3,2,1,0:T(8,128)S(1)} all-to-all(f32[16,2,32,128]{3,2,1,0:T(8,128)S(1)} %shard_map.76), channel_id=1, replica_groups=mesh['z'=16,'ylo'=2,'core'=2,'head'=8] {'ylo','head'}, dimensions={0} | all-to-all | bytes 1048576 | tf_op jit(solution)/shard_map/all_to_all | solution.py:173
  21.3 5.0 %collective-permute-start.1 = (f32[16,2,32,128]{3,2,1,0:T(8,128)S(1)}, f32[16,2,32,128]{3,2,1,0:T(8,128)S(1)}, u32[]{:S(2)}, u32[]{:S(2)}) collective-permute-start(f32[16,2,32,128]{3,2,1,0:T(8,128)S(1)} %all_to_all.20.own_ref), channel_id=1, source_target_pairs={{0,32},{32,64},{64,96},{96,128},{128,160},{160,192},{192,224},{224... | collective-permute-start | bytes 1572872 | tf_op jit(solution)/shard_map/ppermute | solution.py:186
  26.4 1.7 %shard_map.75 = f32[16,4,32,128]{3,2,1,0:T(8,128)} custom-call(f32[32,32,128]{2,1,0:T(8,128)S(1)} %copy-done, f32[32,32,128]{2,1,0:T(8,128)S(1)} %copy-done.1), custom_call_target="tpu_custom_call" | custom-call | tf_op jit(solution)/shard_map/pallas_call | solution.py:162
  28.0 3.7 %all-to-all-start = ((f32[16,4,32,128]{3,2,1,0:T(8,128)}), f32[16,4,32,128]{3,2,1,0:T(8,128)S(1)}, u32[]{:S(2)}, u32[]{:S(2)}) async-start(f32[16,4,32,128]{3,2,1,0:T(8,128)} %shard_map.75), calls=%async_computation | async-start | bytes 2097152 | tf_op jit(solution)/shard_map/all_to_all | solution.py:173
  31.7 1.9 %collective-permute-start = (f32[16,2,32,128]{3,2,1,0:T(8,128)S(1)}, f32[16,2,32,128]{3,2,1,0:T(8,128)S(1)}, u32[]{:S(2)}, u32[]{:S(2)}) collective-permute-start(f32[16,2,32,128]{3,2,1,0:T(8,128)S(1)} %all_to_all.20.own_ref), channel_id=1, source_target_pairs={{0,8},{8,0},{1,9},{9,1},{2,10},{10,2},{3,11},{11,3},{4,12},{12,4},... | collective-permute-start | bytes 1572872 | tf_op jit(solution)/shard_map/ppermute | solution.py:177
  33.6 2.7 %collective-permute-done.1.halo_ref = f32[16,2,32,128]{3,2,1,0:T(8,128)S(1)} collective-permute-done((f32[16,2,32,128]{3,2,1,0:T(8,128)S(1)}, f32[16,2,32,128]{3,2,1,0:T(8,128)S(1)}, u32[]{:S(2)}, u32[]{:S(2)}) %collective-permute-start.1) | collective-permute-done | bytes 524320 | tf_op jit(solution)/shard_map/ppermute | solution.py:186
  36.4 1.9 %collective-permute-start.2 = (f32[16,2,32,128]{3,2,1,0:T(8,128)S(1)}, f32[16,2,32,128]{3,2,1,0:T(8,128)S(1)}, u32[]{:S(2)}, u32[]{:S(2)}) collective-permute-start(f32[16,2,32,128]{3,2,1,0:T(8,128)S(1)} %collective-permute-done.1.halo_ref), channel_id=1, source_target_pairs={{0,8},{8,0},{1,9},{9,1},{2,10},{10,2},{3,11},{11,3},{4,12},{12,4},... | collective-permute-start | bytes 1572872 | tf_op jit(solution)/shard_map/ppermute | solution.py:177
  38.3 9.7 %all-to-all-done.q_ref = f32[16,4,32,128]{3,2,1,0:T(8,128)S(1)} async-done(((f32[16,4,32,128]{3,2,1,0:T(8,128)}), f32[16,4,32,128]{3,2,1,0:T(8,128)S(1)}, u32[]{:S(2)}, u32[]{:S(2)}) %all-to-all-start) | async-done | bytes 1048608 | tf_op jit(solution)/shard_map/all_to_all | solution.py:173
  48.0 0.8 copy-done.2
  49.6 1.0 copy-done.3
  50.6 1.0 copy-done.5
  51.7 14.5 %shard_map.77 = (f32[16,4,32,128]{3,2,1,0:T(8,128)}, f32[16,2,32,128]{3,2,1,0:T(8,128)S(1)}, f32[16,2,32,128]{3,2,1,0:T(8,128)S(1)}, f32[16,2,32,128]{3,2,1,0:T(8,128)S(1)}, f32[16,2,32,128]{3,2,1,0:T(8,128)}) custom-call(f32[16,4,32,128]{3,2,1,0:T(8,128)S(1)} %all-to-all-done.q_ref, f32[16,2,32,128]{3,2,1,0:T(8,128)S(1)} %all_to_all.20.own_ref, ...), custom_call_target="tpu_custom_call" | custom-call | tf_op jit(solution)/shard_map/pallas_call | solution.py:162
  66.9 1.9 %collective-permute-start.4 = (f32[16,2,32,128]{3,2,1,0:T(8,128)}, f32[16,2,32,128]{3,2,1,0:T(8,128)S(1)}, u32[]{:S(2)}, u32[]{:S(2)}) collective-permute-start(f32[16,2,32,128]{3,2,1,0:T(8,128)} %get-tuple-element.19), channel_id=1, source_target_pairs={{0,8},{8,0},{1,9},{9,1},{2,10},{10,2},{3,11},{11,3},{4,12},{12,4},... | collective-permute-start | bytes 1572872 | tf_op jit(solution)/shard_map/ppermute | solution.py:177
  68.9 3.8 %all-to-all-start.2 = ((f32[16,4,32,128]{3,2,1,0:T(8,128)}), f32[16,4,32,128]{3,2,1,0:T(8,128)S(1)}, u32[]{:S(2)}, u32[]{:S(2)}) async-start(f32[16,4,32,128]{3,2,1,0:T(8,128)} %get-tuple-element.13), calls=%async_computation.2 | async-start | bytes 2097152 | tf_op jit(solution)/shard_map/all_to_all | solution.py:173
  72.7 2.4 %collective-permute-start.3 = (f32[16,2,32,128]{3,2,1,0:T(8,128)S(1)}, f32[16,2,32,128]{3,2,1,0:T(8,128)S(1)}, u32[]{:S(2)}, u32[]{:S(2)}) collective-permute-start(f32[16,2,32,128]{3,2,1,0:T(8,128)S(1)} %copy-done.9), channel_id=1, source_target_pairs={{0,8},{8,0},{1,9},{9,1},{2,10},{10,2},{3,11},{11,3},{4,12},{12,4},... | collective-permute-start | bytes 1572872 | tf_op jit(solution)/shard_map/ppermute | solution.py:177
  75.2 1.9 %collective-permute-start.5 = (f32[16,2,32,128]{3,2,1,0:T(8,128)S(1)}, f32[16,2,32,128]{3,2,1,0:T(8,128)S(1)}, u32[]{:S(2)}, u32[]{:S(2)}) collective-permute-start(f32[16,2,32,128]{3,2,1,0:T(8,128)S(1)} %add.10), channel_id=1, source_target_pairs={{32,0},{64,32},{96,64},{128,96},{160,128},{192,160},{224,192},{256... | collective-permute-start | bytes 1572872 | tf_op jit(solution)/shard_map/ppermute | solution.py:205
  77.2 15.0 %collective-permute-done.5 = f32[16,2,32,128]{3,2,1,0:T(8,128)S(1)} collective-permute-done((f32[16,2,32,128]{3,2,1,0:T(8,128)S(1)}, f32[16,2,32,128]{3,2,1,0:T(8,128)S(1)}, u32[]{:S(2)}, u32[]{:S(2)}) %collective-permute-start.5) | collective-permute-done | bytes 524320 | tf_op jit(solution)/shard_map/ppermute | solution.py:205
  92.2 0.9 add_add_fusion
  93.1 7.1 %all-to-all-start.3 = ((f32[16,2,32,128]{3,2,1,0:T(8,128)}), f32[16,2,32,128]{3,2,1,0:T(8,128)S(1)}, u32[]{:S(2)}, u32[]{:S(2)}) async-start(f32[16,2,32,128]{3,2,1,0:T(8,128)} %add_add_fusion), calls=%async_computation.3 | async-start | bytes 1048576 | tf_op jit(solution)/shard_map/all_to_all | solution.py:173
  100.2 2.0 %shard_map.78 = (f32[32,32,128]{2,1,0:T(8,128)}, f32[32,32,128]{2,1,0:T(8,128)}) custom-call(f32[16,4,32,128]{3,2,1,0:T(8,128)S(1)} %all-to-all-done.2.in_ref), custom_call_target="tpu_custom_call" | custom-call | tf_op jit(solution)/shard_map/pallas_call | solution.py:162
  102.2 9.2 %all-to-all-done.3.in_ref = f32[16,2,32,128]{3,2,1,0:T(8,128)S(1)} async-done(((f32[16,2,32,128]{3,2,1,0:T(8,128)}), f32[16,2,32,128]{3,2,1,0:T(8,128)S(1)}, u32[]{:S(2)}, u32[]{:S(2)}) %all-to-all-start.3) | async-done | bytes 524320 | tf_op jit(solution)/shard_map/all_to_all | solution.py:173
  111.4 1.1 shard_map.79
  (22 shorter events, 2.0 us)
Async XLA Ops:
  0.6 1.0 copy-start.6
  1.6 0.9 copy-start.7
  2.8 23.6 %copy-start = (f32[32,32,128]{2,1,0:T(8,128)S(1)}, f32[32,32,128]{2,1,0:T(8,128)}, u32[]{:S(2)}) copy-start(f32[32,32,128]{2,1,0:T(8,128)} %q_ref.1) | copy-start | bytes 1572868
  2.8 23.6 %copy-start.1 = (f32[32,32,128]{2,1,0:T(8,128)S(1)}, f32[32,32,128]{2,1,0:T(8,128)}, u32[]{:S(2)}) copy-start(f32[32,32,128]{2,1,0:T(8,128)} %d_ref.1) | copy-start | bytes 1572868
  21.3 15.0 %collective-permute-start.1 = (f32[16,2,32,128]{3,2,1,0:T(8,128)S(1)}, f32[16,2,32,128]{3,2,1,0:T(8,128)S(1)}, u32[]{:S(2)}, u32[]{:S(2)}) collective-permute-start(f32[16,2,32,128]{3,2,1,0:T(8,128)S(1)} %all_to_all.20.own_ref), channel_id=1, source_target_pairs={{0,32},{32,64},{64,96},{96,128},{128,160},{160,192},{192,224},{224... | collective-permute-start | bytes 1572872 | tf_op jit(solution)/shard_map/ppermute | solution.py:186
  28.0 20.0 %all-to-all-start = ((f32[16,4,32,128]{3,2,1,0:T(8,128)}), f32[16,4,32,128]{3,2,1,0:T(8,128)S(1)}, u32[]{:S(2)}, u32[]{:S(2)}) async-start(f32[16,4,32,128]{3,2,1,0:T(8,128)} %shard_map.75), calls=%async_computation | async-start | bytes 2097152 | tf_op jit(solution)/shard_map/all_to_all | solution.py:173
  31.7 16.3 %collective-permute-start = (f32[16,2,32,128]{3,2,1,0:T(8,128)S(1)}, f32[16,2,32,128]{3,2,1,0:T(8,128)S(1)}, u32[]{:S(2)}, u32[]{:S(2)}) collective-permute-start(f32[16,2,32,128]{3,2,1,0:T(8,128)S(1)} %all_to_all.20.own_ref), channel_id=1, source_target_pairs={{0,8},{8,0},{1,9},{9,1},{2,10},{10,2},{3,11},{11,3},{4,12},{12,4},... | collective-permute-start | bytes 1572872 | tf_op jit(solution)/shard_map/ppermute | solution.py:177
  36.4 12.4 %collective-permute-start.2 = (f32[16,2,32,128]{3,2,1,0:T(8,128)S(1)}, f32[16,2,32,128]{3,2,1,0:T(8,128)S(1)}, u32[]{:S(2)}, u32[]{:S(2)}) collective-permute-start(f32[16,2,32,128]{3,2,1,0:T(8,128)S(1)} %collective-permute-done.1.halo_ref), channel_id=1, source_target_pairs={{0,8},{8,0},{1,9},{9,1},{2,10},{10,2},{3,11},{11,3},{4,12},{12,4},... | collective-permute-start | bytes 1572872 | tf_op jit(solution)/shard_map/ppermute | solution.py:177
  48.0 0.8 copy-start.2
  48.8 0.8 copy-start.4
  49.6 1.0 copy-start.3
  50.6 1.0 copy-start.5
  66.2 0.8 copy-start.8
  66.9 8.2 %collective-permute-start.4 = (f32[16,2,32,128]{3,2,1,0:T(8,128)}, f32[16,2,32,128]{3,2,1,0:T(8,128)S(1)}, u32[]{:S(2)}, u32[]{:S(2)}) collective-permute-start(f32[16,2,32,128]{3,2,1,0:T(8,128)} %get-tuple-element.19), channel_id=1, source_target_pairs={{0,8},{8,0},{1,9},{9,1},{2,10},{10,2},{3,11},{11,3},{4,12},{12,4},... | collective-permute-start | bytes 1572872 | tf_op jit(solution)/shard_map/ppermute | solution.py:177
  68.9 3.8 %copy-start.9 = (f32[16,2,32,128]{3,2,1,0:T(8,128)S(1)}, f32[16,2,32,128]{3,2,1,0:T(8,128)}, u32[]{:S(2)}) copy-start(f32[16,2,32,128]{3,2,1,0:T(8,128)} %copy-done.8) | copy-start | bytes 1572868
  68.9 24.2 %all-to-all-start.2 = ((f32[16,4,32,128]{3,2,1,0:T(8,128)}), f32[16,4,32,128]{3,2,1,0:T(8,128)S(1)}, u32[]{:S(2)}, u32[]{:S(2)}) async-start(f32[16,4,32,128]{3,2,1,0:T(8,128)} %get-tuple-element.13), calls=%async_computation.2 | async-start | bytes 2097152 | tf_op jit(solution)/shard_map/all_to_all | solution.py:173
  72.7 4.5 %collective-permute-start.3 = (f32[16,2,32,128]{3,2,1,0:T(8,128)S(1)}, f32[16,2,32,128]{3,2,1,0:T(8,128)S(1)}, u32[]{:S(2)}, u32[]{:S(2)}) collective-permute-start(f32[16,2,32,128]{3,2,1,0:T(8,128)S(1)} %copy-done.9), channel_id=1, source_target_pairs={{0,8},{8,0},{1,9},{9,1},{2,10},{10,2},{3,11},{11,3},{4,12},{12,4},... | collective-permute-start | bytes 1572872 | tf_op jit(solution)/shard_map/ppermute | solution.py:177
  75.2 16.9 %collective-permute-start.5 = (f32[16,2,32,128]{3,2,1,0:T(8,128)S(1)}, f32[16,2,32,128]{3,2,1,0:T(8,128)S(1)}, u32[]{:S(2)}, u32[]{:S(2)}) collective-permute-start(f32[16,2,32,128]{3,2,1,0:T(8,128)S(1)} %add.10), channel_id=1, source_target_pairs={{32,0},{64,32},{96,64},{128,96},{160,128},{192,160},{224,192},{256... | collective-permute-start | bytes 1572872 | tf_op jit(solution)/shard_map/ppermute | solution.py:205
  93.1 18.3 %all-to-all-start.3 = ((f32[16,2,32,128]{3,2,1,0:T(8,128)}), f32[16,2,32,128]{3,2,1,0:T(8,128)S(1)}, u32[]{:S(2)}, u32[]{:S(2)}) async-start(f32[16,2,32,128]{3,2,1,0:T(8,128)} %add_add_fusion), calls=%async_computation.3 | async-start | bytes 1048576 | tf_op jit(solution)/shard_map/all_to_all | solution.py:173

commit v2 on v1

v2 whole, which is shorter than its diff:
```python
import jax
import jax.numpy as jnp
from jax import lax
from jax.experimental import pallas as pl
from jax.experimental.pallas import tpu as pltpu
from jax.sharding import Mesh, PartitionSpec as P

WINDOW = 1024
HEADS = 32
GROUPS = 16
HEAD_DIM = 128
ROWS = 32
BLOCK = 256
PEERS = 16
PLANE_AXES = ("ylo", "head")

query_scale = 168.0 ** (-0.5)
LOG2E = 1.4426950408889634
LN2 = 0.6931471805599453
f32 = jnp.float32
bf16 = jnp.bfloat16

VMEM = pl.BlockSpec(memory_space=pltpu.VMEM)


def params(vmem):
    return pltpu.CompilerParams(vmem_limit_bytes=vmem * 1024 * 1024)


def pack_kv_kernel(k_ref, v_ref, out_ref):
    for g in range(GROUPS):
        out_ref[g, 0] = k_ref[:, g, :]
        out_ref[g, 1] = v_ref[:, g, :]


def pack_q_kernel(q_ref, d_ref, out_ref):
    for g in range(GROUPS):
        for h in range(2):
            out_ref[g, h] = q_ref[:, 2 * g + h, :]
            out_ref[g, 2 + h] = d_ref[:, 2 * g + h, :]


def unpack_kv_kernel(in_ref, k_ref, v_ref):
    for g in range(GROUPS):
        k_ref[:, g, :] = in_ref[g, 0]
        v_ref[:, g, :] = in_ref[g, 1]


def unpack_q_kernel(in_ref, a_ref, q_ref):
    for g in range(GROUPS):
        for h in range(2):
            a_ref[:, 2 * g + h, :] = in_ref[g, h]
            q_ref[:, 2 * g + h, :] = in_ref[g, 2 + h]


def split(x):
    hi = x.astype(bf16)
    lo = (x - hi.astype(f32)).astype(bf16)
    return hi, lo


def dot(a, b):
    return lax.dot_general(a, b, (((1,), (0,)), ((), ())), preferred_element_type=f32)


SPAN = 5 * BLOCK


def attend_kernel(
    rows_in, own_in, halo_in, other_in,
    out_buf, gmine, gother,
    kcat, vcat, kt, vt, s_ref, wcat, dscat, qw_ref, dw_ref,
):
    z = lax.axis_index("z")
    core = lax.axis_index("core")
    for r in range(7):
        here = pl.ds(r * BLOCK, BLOCK)
        for i, cat, tr in ((0, kcat, kt), (1, vcat, vt)):
            ref, at = (other_in, 8 * (r // 2)) if r % 2 else (halo_in if r < 4 else own_in, 8 * (r // 2 % 2))
            x = ref[at : at + 8, i]
            x = x.reshape(BLOCK, HEAD_DIM)
            hi, lo = split(x)
            cat[here, :HEAD_DIM] = hi
            cat[here, HEAD_DIM : 2 * HEAD_DIM] = lo
            cat[here, 2 * HEAD_DIM :] = hi
            thi, tlo = split(x.T)
            tr[:HEAD_DIM, here] = thi
            tr[HEAD_DIM:, here] = tlo
    key_iota = lax.broadcasted_iota(jnp.int32, (BLOCK, BLOCK), 0)
    query_iota = lax.broadcasted_iota(jnp.int32, (BLOCK, BLOCK), 1)
    later = key_iota > query_iota

    def exists(y, b):
        return (z * 4 + 2 * y + core + b - 4) >= 0

    state = {}

    def scores(y, h):
        q = rows_in[8 * y : 8 * y + 8, h].reshape(BLOCK, HEAD_DIM) * (query_scale * LOG2E)
        qt_hi, qt_lo = split(q.T)
        q_hi, q_lo = split(q)
        qt3 = jnp.concatenate([qt_hi, qt_hi, qt_lo], axis=0)
        row_max = None
        for b in range(5):
            here = pl.ds((2 * y + b) * BLOCK, BLOCK)
            s = dot(kcat[here, :], qt3)
            if b == 0:
                s = jnp.where(later, s, -jnp.inf)
            if b == 4:
                s = jnp.where(later, -jnp.inf, s)
            s_ref[2 * y + h, b] = s
            m = jnp.max(s, axis=0, keepdims=True)
            if b < 4:
                m = jnp.where(exists(y, b), m, -jnp.inf)
            row_max = m if row_max is None else jnp.maximum(row_max, m)
        qw_ref[y, h * BLOCK : (h + 1) * BLOCK, :] = jnp.concatenate([q_hi, q_lo], axis=1)
        state[y, h] = row_max

    def weigh(y, h):
        row_max = state[y, h]
        i = 2 * y + h
        total = None
        for b in range(5):
            shift = row_max if b == 4 else jnp.where(exists(y, b), row_max, jnp.inf)
            w = jnp.exp2(s_ref[i, b] - shift)
            t = jnp.sum(w, axis=0, keepdims=True)
            total = t if total is None else total + t
            hi, lo = split(w)
            s_ref[i, b] = w
            wcat[y, b * BLOCK : (b + 1) * BLOCK, h * 512 : h * 512 + 256] = hi
            wcat[y, b * BLOCK : (b + 1) * BLOCK, h * 512 + 256 : h * 512 + 512] = lo
        vts = vt[:, 2 * y * BLOCK : 2 * y * BLOCK + SPAN]
        both = dot(vts, wcat[y, :, h * 512 : h * 512 + 256])
        at_sum = both[:HEAD_DIM] + both[HEAD_DIM:] + dot(vts[:HEAD_DIM], wcat[y, :, h * 512 + 256 : h * 512 + 512])
        inverse = 1.0 / total
        at_sum = at_sum * inverse
        out_buf[8 * y : 8 * y + 8, h] = at_sum.T.reshape(8, ROWS, HEAD_DIM)
        dt = rows_in[8 * y : 8 * y + 8, 2 + h].reshape(BLOCK, HEAD_DIM).T * inverse
        row_dots = jnp.sum(dt * at_sum, axis=0, keepdims=True)
        d_hi, d_lo = split(dt.T)
        dw_ref[y, h * BLOCK : (h + 1) * BLOCK, :] = jnp.concatenate([d_hi, d_lo], axis=1)
        state[y, h] = (row_dots, dt)

    def grads(y, h):
        row_dots, dt = state[y, h]
        i = 2 * y + h
        dt_hi, dt_lo = split(dt)
        dt3 = jnp.concatenate([dt_hi, dt_hi, dt_lo], axis=0)
        for b in range(5):
            here = pl.ds((2 * y + b) * BLOCK, BLOCK)
            dp = dot(vcat[here, :], dt3)
            hi, lo = split(s_ref[i, b] * (dp - row_dots))
            dscat[y, b * BLOCK : (b + 1) * BLOCK, h * 512 : h * 512 + 256] = hi
            dscat[y, b * BLOCK : (b + 1) * BLOCK, h * 512 + 256 : h * 512 + 512] = lo
        kts = kt[:, 2 * y * BLOCK : 2 * y * BLOCK + SPAN]
        both = dot(kts, dscat[y, :, h * 512 : h * 512 + 256])
        dq = both[:HEAD_DIM] + both[HEAD_DIM:] + dot(kts[:HEAD_DIM], dscat[y, :, h * 512 + 256 : h * 512 + 512])
        dq = dq * query_scale
        out_buf[8 * y : 8 * y + 8, 2 + h] = dq.T.reshape(8, ROWS, HEAD_DIM)

    def key_sums(y):
        for kind, cat, weight_ref in ((0, dscat, qw_ref), (1, wcat, dw_ref)):
            zero = jnp.zeros((BLOCK, HEAD_DIM), bf16)
            parts = []
            for h in range(2):
                both = weight_ref[y, h * BLOCK : (h + 1) * BLOCK, :]
                parts += [both, jnp.concatenate([both[:, :HEAD_DIM], zero], axis=1)]
            weights = jnp.concatenate(parts, axis=0)
            for b in range(5):
                both = dot(cat[y, b * BLOCK : (b + 1) * BLOCK, :], weights)
                part = both[:, :HEAD_DIM] + both[:, HEAD_DIM:]
                if kind == 0:
                    part = part * LN2
                r = 2 * y + b
                at = pl.ds(8 * (r // 2), 8) if r % 2 == 0 else pl.ds(pl.multiple_of(8 * (r // 2 + core), 8), 8)
                ref = gmine if r % 2 == 0 else gother
                part = part.reshape(8, ROWS, HEAD_DIM)
                if y == 1 and b < 3:
                    part = part + ref[at, kind]
                ref[at, kind] = part

    unused = pl.ds(pl.multiple_of(24 * (1 - core), 8), 8)
    gother[unused, :] = jnp.zeros((8, 2, ROWS, HEAD_DIM), f32)
    scores(0, 0)
    scores(0, 1)
    weigh(0, 0)
    scores(1, 0)
    weigh(0, 1)
    grads(0, 0)
    scores(1, 1)
    weigh(1, 0)
    grads(0, 1)
    key_sums(0)
    weigh(1, 1)
    grads(1, 0)
    grads(1, 1)
    key_sums(1)


def shape(*dims):
    return jax.ShapeDtypeStruct(dims, f32)


def call(kernel, outs, ins, scratch=(), cost=1, vmem=16):
    return pl.pallas_call(
        kernel,
        out_shape=outs,
        in_specs=[VMEM] * len(ins),
        out_specs=[VMEM] * len(outs) if isinstance(outs, tuple) else VMEM,
        scratch_shapes=list(scratch),
        compiler_params=params(vmem),
        cost_estimate=pl.CostEstimate(flops=cost * 1_000_000_000, bytes_accessed=cost * 3_000_000, transcendentals=0),
    )(*ins)


def exchanged(x):
    return lax.all_to_all(x, PLANE_AXES, 0, 0, tiled=True)


def swapped(x):
    return lax.ppermute(x, "core", [(0, 1), (1, 0)])


def attend_call(rows, own, halo, other):
    scratch = (
        pltpu.VMEM((7 * BLOCK, 3 * HEAD_DIM), bf16),
        pltpu.VMEM((7 * BLOCK, 3 * HEAD_DIM), bf16),
        pltpu.VMEM((2 * HEAD_DIM, 7 * BLOCK), bf16),
        pltpu.VMEM((2 * HEAD_DIM, 7 * BLOCK), bf16),
        pltpu.VMEM((4, 5, BLOCK, BLOCK), f32),
        pltpu.VMEM((2, SPAN, 4 * BLOCK), bf16),
        pltpu.VMEM((2, SPAN, 4 * BLOCK), bf16),
        pltpu.VMEM((2, 2 * BLOCK, 2 * HEAD_DIM), bf16),
        pltpu.VMEM((2, 2 * BLOCK, 2 * HEAD_DIM), bf16),
    )
    kv_shape = shape(2 * PEERS, 2, ROWS, HEAD_DIM)
    outs = (shape(PEERS, 4, ROWS, HEAD_DIM), kv_shape, kv_shape)
    return call(attend_kernel, outs, (rows, own, halo, other), scratch, cost=8, vmem=36)


def per_device(queries, keys, values, out_grad):
    planes = lax.axis_size("z")
    kv_shape = shape(PEERS, 2, ROWS, HEAD_DIM)
    q_shape = shape(PEERS, 4, ROWS, HEAD_DIM)
    own = exchanged(call(pack_kv_kernel, kv_shape, (keys, values), cost=1))
    packed = call(pack_q_kernel, q_shape, (queries, out_grad), cost=1)
    own, packed = lax.optimization_barrier((own, packed))
    rows = exchanged(packed)
    halo = lax.ppermute(own, "z", [(i, i + 1) for i in range(planes - 1)])
    ownx = swapped(own)
    halox = swapped(halo)
    half = PEERS // 2
    rows, ownx, halox = lax.optimization_barrier((rows, ownx, halox))
    other = jnp.where(
        lax.axis_index("core") == 0,
        jnp.concatenate([halox, ownx[:half]], axis=0),
        jnp.concatenate([halox[half:], ownx], axis=0),
    )
    out, gmine, gother = attend_call(rows, own, halo, other)
    back = exchanged(out)
    received = swapped(gother)
    ghalo = gmine[:PEERS] + received[:PEERS]
    returned = lax.ppermute(ghalo, "z", [(i + 1, i) for i in range(planes - 1)])
    total = gmine[PEERS:] + received[PEERS:] + returned
    kv_back = exchanged(total)
    attention, query_grad = call(unpack_q_kernel, (shape(ROWS, HEADS, HEAD_DIM),) * 2, (back,), cost=1)
    key_grad, value_grad = call(unpack_kv_kernel, (shape(ROWS, GROUPS, HEAD_DIM),) * 2, (kv_back,), cost=1)
    return attention, query_grad, key_grad, value_grad


def solution(mesh):
    inner = Mesh(mesh.devices.reshape(-1, 2, 2, mesh.shape["head"]), ("z", "ylo", "core", "head"))
    spec = P(("z", "ylo", "core", "head"), None, None)
    return jax.shard_map(per_device, mesh=inner, in_specs=(spec,) * 4, out_specs=(spec,) * 4, check_vma=False)
```

time: 113 us -> 101 us (0.89)
  blocking collectives: 18.5 us -> 0 us
  waiting for transfers between devices: 36.6 us -> 48.4 us
  local copies, waits for them, and re-layouts: 6.37 us -> 1.94 us
  Pallas kernels: 19.5 us -> 15.5 us
  starting transfers between devices: 29.7 us -> 32.5 us
    all_to_all x1 -> x0, blocking collectives: 18.5 us -> none  [exchanged(): return lax.all_to_all(x, PLANE_AXES, 0, 0, tiled=True)]
    all_to_all x3 -> x4, waiting for transfers between devices: 18.9 us -> 28.5 us  [exchanged(): return lax.all_to_all(x, PLANE_AXES, 0, 0, tiled=True)]
    all_to_all x3 -> x4, starting transfers between devices: 14.6 us -> 19.8 us  [exchanged(): return lax.all_to_all(x, PLANE_AXES, 0, 0, tiled=True)]
    unnamed x20 -> x8, local copies, waits for them, and re-layouts: 6.37 us -> 1.9 us
    pallas_call x5, Pallas kernels: 19.5 us -> 15.5 us  [call(): pl.pallas_call(kernel, out_shape=outs, in_specs=[VMEM] * len(ins), out_sp...]
    ppermute x4 -> x3, starting transfers between devices: 8.14 us -> 5.74 us  [swapped(): return lax.ppermute(x, 'core', [(0, 1), (1, 0)])]
    ppermute x1, waiting for transfers between devices: 2.74 us -> 4.41 us  [per_device(): halo = lax.ppermute(own, 'z', [(i, i + 1) for i in range(planes - 1)])]
  transfers between devices with their start and end apart: 9 -> 9, of which waited for: 4 -> 6; matrix products, arithmetic and copies ran while one was open for 1% -> 1% of each run, Pallas kernels for 3% -> 4%
where the time goes in v2:
time: 101 us; the launch traced here: 100 us
  waiting for transfers between devices  48.4 us (48%)
  starting transfers between devices  32.5 us (32%)
  Pallas kernels  15.5 us (15%)
  local copies, waits for them, and re-layouts  1.94 us (2%)
  other arithmetic  1.2 us (1%)
    all_to_all x4, waiting for transfers between devices, exchanged(): return lax.all_to_all(x, PLANE_AXES, 0, 0, tiled=True)  28.5 us
    all_to_all x4, starting transfers between devices, exchanged(): return lax.all_to_all(x, PLANE_AXES, 0, 0, tiled=True)  19.8 us
    ppermute x1, waiting for transfers between devices, per_device(): returned = lax.ppermute(ghalo, 'z', [(i + 1, i) for i in range(planes - 1)])  15.5 us
    pallas_call x5, Pallas kernels, call(): pl.pallas_call(kernel, out_shape=outs, in_specs=[VMEM] * len(ins), out_sp...  15.5 us
    ppermute x3, starting transfers between devices, swapped(): return lax.ppermute(x, 'core', [(0, 1), (1, 0)])  5.74 us
    ppermute x1, starting transfers between devices, per_device(): halo = lax.ppermute(own, 'z', [(i, i + 1) for i in range(planes - 1)])  5.02 us
    ppermute x1, waiting for transfers between devices, per_device(): halo = lax.ppermute(own, 'z', [(i, i + 1) for i in range(planes - 1)])  4.41 us
  transfers between devices with their start and end apart: 9, of which 6 were waited for; matrix products, arithmetic and copies ran while one was open for 1% of the time, Pallas kernels for 4%

profile of v2, /device:TPU:224, one launch (start us, length us, event | category | flops | bytes accessed | tf_op | source)
XLA Modules:
  0.0 100.3 jit_solution(14769300383259370397)
XLA Ops:
  0.6 0.9 copy-done.2
  1.6 0.9 copy-done.3
  2.5 1.1 %shard_map.75 = f32[16,2,32,128]{3,2,1,0:T(8,128)} custom-call(f32[32,16,128]{2,1,0:T(8,128)S(1)} %copy-done.2, f32[32,16,128]{2,1,0:T(8,128)S(1)} %copy-done.3), custom_call_target="tpu_custom_call" | custom-call | flops 1000000000 | bytes 3000000 | tf_op jit(solution)/shard_map/pallas_call | solution.py:205
  3.6 7.2 %all-to-all-start = ((f32[16,2,32,128]{3,2,1,0:T(8,128)}), f32[16,2,32,128]{3,2,1,0:T(8,128)S(1)}, u32[]{:S(2)}, u32[]{:S(2)}) async-start(f32[16,2,32,128]{3,2,1,0:T(8,128)} %shard_map.75), calls=%async_computation | async-start | bytes 1048576 | tf_op jit(solution)/shard_map/all_to_all | solution.py:217
  10.8 1.6 %shard_map.76 = f32[16,4,32,128]{3,2,1,0:T(8,128)} custom-call(f32[32,32,128]{2,1,0:T(8,128)S(1)} %copy-done, f32[32,32,128]{2,1,0:T(8,128)S(1)} %copy-done.1), custom_call_target="tpu_custom_call" | custom-call | flops 1000000000 | bytes 3000000 | tf_op jit(solution)/shard_map/pallas_call | solution.py:205
  12.4 9.9 %all-to-all-done.own_in = f32[16,2,32,128]{3,2,1,0:T(8,128)S(1)} async-done(((f32[16,2,32,128]{3,2,1,0:T(8,128)}), f32[16,2,32,128]{3,2,1,0:T(8,128)S(1)}, u32[]{:S(2)}, u32[]{:S(2)}) %all-to-all-start) | async-done | bytes 524320 | tf_op jit(solution)/shard_map/all_to_all | solution.py:217
  22.3 5.0 %collective-permute-start.1 = (f32[16,2,32,128]{3,2,1,0:T(8,128)S(1)}, f32[16,2,32,128]{3,2,1,0:T(8,128)S(1)}, u32[]{:S(2)}, u32[]{:S(2)}) collective-permute-start(f32[16,2,32,128]{3,2,1,0:T(8,128)S(1)} %all-to-all-done.own_in), channel_id=1, source_target_pairs={{0,32},{32,64},{64,96},{96,128},{128,160},{160,192},{192,224},{224... | collective-permute-start | bytes 1572872 | tf_op jit(solution)/shard_map/ppermute | solution.py:249
  27.3 3.7 %all-to-all-start.1 = ((f32[16,4,32,128]{3,2,1,0:T(8,128)}), f32[16,4,32,128]{3,2,1,0:T(8,128)S(1)}, u32[]{:S(2)}, u32[]{:S(2)}) async-start(f32[16,4,32,128]{3,2,1,0:T(8,128)} %shard_map.76), calls=%async_computation.1 | async-start | bytes 2097152 | tf_op jit(solution)/shard_map/all_to_all | solution.py:217
  31.0 1.9 %collective-permute-start = (f32[16,2,32,128]{3,2,1,0:T(8,128)S(1)}, f32[16,2,32,128]{3,2,1,0:T(8,128)S(1)}, u32[]{:S(2)}, u32[]{:S(2)}) collective-permute-start(f32[16,2,32,128]{3,2,1,0:T(8,128)S(1)} %all-to-all-done.own_in), channel_id=1, source_target_pairs={{0,8},{8,0},{1,9},{9,1},{2,10},{10,2},{3,11},{11,3},{4,12},{12,4},... | collective-permute-start | bytes 1572872 | tf_op jit(solution)/shard_map/ppermute | solution.py:221
  32.9 4.4 %collective-permute-done.1.halo_in = f32[16,2,32,128]{3,2,1,0:T(8,128)S(1)} collective-permute-done((f32[16,2,32,128]{3,2,1,0:T(8,128)S(1)}, f32[16,2,32,128]{3,2,1,0:T(8,128)S(1)}, u32[]{:S(2)}, u32[]{:S(2)}) %collective-permute-start.1) | collective-permute-done | bytes 524320 | tf_op jit(solution)/shard_map/ppermute | solution.py:249
  37.4 1.9 %collective-permute-start.2 = (f32[16,2,32,128]{3,2,1,0:T(8,128)S(1)}, f32[16,2,32,128]{3,2,1,0:T(8,128)S(1)}, u32[]{:S(2)}, u32[]{:S(2)}) collective-permute-start(f32[16,2,32,128]{3,2,1,0:T(8,128)S(1)} %collective-permute-done.1.halo_in), channel_id=1, source_target_pairs={{0,8},{8,0},{1,9},{9,1},{2,10},{10,2},{3,11},{11,3},{4,12},{12,4},... | collective-permute-start | bytes 1572872 | tf_op jit(solution)/shard_map/ppermute | solution.py:221
  39.3 8.0 %all-to-all-done.1.rows_in = f32[16,4,32,128]{3,2,1,0:T(8,128)S(1)} async-done(((f32[16,4,32,128]{3,2,1,0:T(8,128)}), f32[16,4,32,128]{3,2,1,0:T(8,128)S(1)}, u32[]{:S(2)}, u32[]{:S(2)}) %all-to-all-start.1) | async-done | bytes 1048608 | tf_op jit(solution)/shard_map/all_to_all | solution.py:217
  47.4 0.1 maximum_select_fusion.other_in
  47.5 9.7 %shard_map.77 = (f32[16,4,32,128]{3,2,1,0:T(8,128)}, f32[32,2,32,128]{3,2,1,0:T(8,128)S(1)}, f32[32,2,32,128]{3,2,1,0:T(8,128)}) custom-call(f32[16,4,32,128]{3,2,1,0:T(8,128)S(1)} %all-to-all-done.1.rows_in, f32[16,2,32,128]{3,2,1,0:T(8,128)S(1)} %all-to-all-done.own_in, f32[16,2,32,128]{3,2,1,0:T(8,128)S(1)} %collective-permute-done.1.halo_in, ...), custom_call_target="tpu_custom_call" | custom-call | flops 8000000000 | bytes 24000000 | tf_op jit(solution)/shard_map/pallas_call | solution.py:205
  57.2 1.9 %collective-permute-start.3 = (f32[32,2,32,128]{3,2,1,0:T(8,128)}, f32[32,2,32,128]{3,2,1,0:T(8,128)S(1)}, u32[]{:S(2)}, u32[]{:S(2)}) collective-permute-start(f32[32,2,32,128]{3,2,1,0:T(8,128)} %get-tuple-element.25), channel_id=1, source_target_pairs={{0,8},{8,0},{1,9},{9,1},{2,10},{10,2},{3,11},{11,3},{4,12},{12,4},... | collective-permute-start | bytes 3145736 | tf_op jit(solution)/shard_map/ppermute | solution.py:221
  59.1 3.7 %all-to-all-start.2 = ((f32[16,4,32,128]{3,2,1,0:T(8,128)}), f32[16,4,32,128]{3,2,1,0:T(8,128)S(1)}, u32[]{:S(2)}, u32[]{:S(2)}) async-start(f32[16,4,32,128]{3,2,1,0:T(8,128)} %get-tuple-element.21), calls=%async_computation.2 | async-start | bytes 2097152 | tf_op jit(solution)/shard_map/all_to_all | solution.py:217
  62.9 1.9 %collective-permute-start.4 = (f32[16,2,32,128]{3,2,1,0:T(8,128)S(1)}, f32[16,2,32,128]{3,2,1,0:T(8,128)S(1)}, u32[]{:S(2)}, u32[]{:S(2)}) collective-permute-start(f32[16,2,32,128]{3,2,1,0:T(8,128)S(1)} %slice_add_fusion), channel_id=1, source_target_pairs={{32,0},{64,32},{96,64},{128,96},{160,128},{192,160},{224,192},{256... | collective-permute-start | bytes 1572872 | tf_op jit(solution)/shard_map/ppermute | solution.py:263
  64.8 15.5 %collective-permute-done.4 = f32[16,2,32,128]{3,2,1,0:T(8,128)S(1)} collective-permute-done((f32[16,2,32,128]{3,2,1,0:T(8,128)S(1)}, f32[16,2,32,128]{3,2,1,0:T(8,128)S(1)}, u32[]{:S(2)}, u32[]{:S(2)}) %collective-permute-start.4) | collective-permute-done | bytes 524320 | tf_op jit(solution)/shard_map/ppermute | solution.py:263
  80.3 1.0 fusion
  81.3 1.5 %all-to-all-done.2.in_ref = f32[16,4,32,128]{3,2,1,0:T(8,128)S(1)} async-done(((f32[16,4,32,128]{3,2,1,0:T(8,128)}), f32[16,4,32,128]{3,2,1,0:T(8,128)S(1)}, u32[]{:S(2)}, u32[]{:S(2)}) %all-to-all-start.2) | async-done | bytes 1048608 | tf_op jit(solution)/shard_map/all_to_all | solution.py:217
  82.8 5.3 %all-to-all-start.3 = ((f32[16,2,32,128]{3,2,1,0:T(8,128)}), f32[16,2,32,128]{3,2,1,0:T(8,128)S(1)}, u32[]{:S(2)}, u32[]{:S(2)}) async-start(f32[16,2,32,128]{3,2,1,0:T(8,128)} %fusion), calls=%async_computation.3 | async-start | bytes 1048576 | tf_op jit(solution)/shard_map/all_to_all | solution.py:217
  88.1 2.0 %shard_map.78 = (f32[32,32,128]{2,1,0:T(8,128)}, f32[32,32,128]{2,1,0:T(8,128)}) custom-call(f32[16,4,32,128]{3,2,1,0:T(8,128)S(1)} %all-to-all-done.2.in_ref), custom_call_target="tpu_custom_call" | custom-call | flops 1000000000 | bytes 3000000 | tf_op jit(solution)/shard_map/pallas_call | solution.py:205
  90.2 9.1 %all-to-all-done.3.in_ref = f32[16,2,32,128]{3,2,1,0:T(8,128)S(1)} async-done(((f32[16,2,32,128]{3,2,1,0:T(8,128)}), f32[16,2,32,128]{3,2,1,0:T(8,128)S(1)}, u32[]{:S(2)}, u32[]{:S(2)}) %all-to-all-start.3) | async-done | bytes 524320 | tf_op jit(solution)/shard_map/all_to_all | solution.py:217
  99.2 1.1 %shard_map.79 = (f32[32,16,128]{2,1,0:T(8,128)}, f32[32,16,128]{2,1,0:T(8,128)}) custom-call(f32[16,2,32,128]{3,2,1,0:T(8,128)S(1)} %all-to-all-done.3.in_ref), custom_call_target="tpu_custom_call" | custom-call | flops 1000000000 | bytes 3000000 | tf_op jit(solution)/shard_map/pallas_call | solution.py:205
  (12 shorter events, 0.1 us)
Async XLA Ops:
  0.6 1.0 copy-start.2
  1.6 0.9 copy-start.3
  3.6 7.2 %copy-start = (f32[32,32,128]{2,1,0:T(8,128)S(1)}, f32[32,32,128]{2,1,0:T(8,128)}, u32[]{:S(2)}) copy-start(f32[32,32,128]{2,1,0:T(8,128)} %q_ref.1) | copy-start | bytes 1572868
  3.6 7.2 %copy-start.1 = (f32[32,32,128]{2,1,0:T(8,128)S(1)}, f32[32,32,128]{2,1,0:T(8,128)}, u32[]{:S(2)}) copy-start(f32[32,32,128]{2,1,0:T(8,128)} %d_ref.1) | copy-start | bytes 1572868
  3.6 18.7 %all-to-all-start = ((f32[16,2,32,128]{3,2,1,0:T(8,128)}), f32[16,2,32,128]{3,2,1,0:T(8,128)S(1)}, u32[]{:S(2)}, u32[]{:S(2)}) async-start(f32[16,2,32,128]{3,2,1,0:T(8,128)} %shard_map.75), calls=%async_computation | async-start | bytes 1048576 | tf_op jit(solution)/shard_map/all_to_all | solution.py:217
  22.3 15.0 %collective-permute-start.1 = (f32[16,2,32,128]{3,2,1,0:T(8,128)S(1)}, f32[16,2,32,128]{3,2,1,0:T(8,128)S(1)}, u32[]{:S(2)}, u32[]{:S(2)}) collective-permute-start(f32[16,2,32,128]{3,2,1,0:T(8,128)S(1)} %all-to-all-done.own_in), channel_id=1, source_target_pairs={{0,32},{32,64},{64,96},{96,128},{128,160},{160,192},{192,224},{224... | collective-permute-start | bytes 1572872 | tf_op jit(solution)/shard_map/ppermute | solution.py:249
  27.3 20.0 %all-to-all-start.1 = ((f32[16,4,32,128]{3,2,1,0:T(8,128)}), f32[16,4,32,128]{3,2,1,0:T(8,128)S(1)}, u32[]{:S(2)}, u32[]{:S(2)}) async-start(f32[16,4,32,128]{3,2,1,0:T(8,128)} %shard_map.76), calls=%async_computation.1 | async-start | bytes 2097152 | tf_op jit(solution)/shard_map/all_to_all | solution.py:217
  31.0 8.3 %collective-permute-start = (f32[16,2,32,128]{3,2,1,0:T(8,128)S(1)}, f32[16,2,32,128]{3,2,1,0:T(8,128)S(1)}, u32[]{:S(2)}, u32[]{:S(2)}) collective-permute-start(f32[16,2,32,128]{3,2,1,0:T(8,128)S(1)} %all-to-all-done.own_in), channel_id=1, source_target_pairs={{0,8},{8,0},{1,9},{9,1},{2,10},{10,2},{3,11},{11,3},{4,12},{12,4},... | collective-permute-start | bytes 1572872 | tf_op jit(solution)/shard_map/ppermute | solution.py:221
  37.4 10.0 %collective-permute-start.2 = (f32[16,2,32,128]{3,2,1,0:T(8,128)S(1)}, f32[16,2,32,128]{3,2,1,0:T(8,128)S(1)}, u32[]{:S(2)}, u32[]{:S(2)}) collective-permute-start(f32[16,2,32,128]{3,2,1,0:T(8,128)S(1)} %collective-permute-done.1.halo_in), channel_id=1, source_target_pairs={{0,8},{8,0},{1,9},{9,1},{2,10},{10,2},{3,11},{11,3},{4,12},{12,4},... | collective-permute-start | bytes 1572872 | tf_op jit(solution)/shard_map/ppermute | solution.py:221
  57.2 5.6 %collective-permute-start.3 = (f32[32,2,32,128]{3,2,1,0:T(8,128)}, f32[32,2,32,128]{3,2,1,0:T(8,128)S(1)}, u32[]{:S(2)}, u32[]{:S(2)}) collective-permute-start(f32[32,2,32,128]{3,2,1,0:T(8,128)} %get-tuple-element.25), channel_id=1, source_target_pairs={{0,8},{8,0},{1,9},{9,1},{2,10},{10,2},{3,11},{11,3},{4,12},{12,4},... | collective-permute-start | bytes 3145736 | tf_op jit(solution)/shard_map/ppermute | solution.py:221
  59.1 23.7 %all-to-all-start.2 = ((f32[16,4,32,128]{3,2,1,0:T(8,128)}), f32[16,4,32,128]{3,2,1,0:T(8,128)S(1)}, u32[]{:S(2)}, u32[]{:S(2)}) async-start(f32[16,4,32,128]{3,2,1,0:T(8,128)} %get-tuple-element.21), calls=%async_computation.2 | async-start | bytes 2097152 | tf_op jit(solution)/shard_map/all_to_all | solution.py:217
  62.9 17.4 %collective-permute-start.4 = (f32[16,2,32,128]{3,2,1,0:T(8,128)S(1)}, f32[16,2,32,128]{3,2,1,0:T(8,128)S(1)}, u32[]{:S(2)}, u32[]{:S(2)}) collective-permute-start(f32[16,2,32,128]{3,2,1,0:T(8,128)S(1)} %slice_add_fusion), channel_id=1, source_target_pairs={{32,0},{64,32},{96,64},{128,96},{160,128},{192,160},{224,192},{256... | collective-permute-start | bytes 1572872 | tf_op jit(solution)/shard_map/ppermute | solution.py:263
  82.8 16.4 %all-to-all-start.3 = ((f32[16,2,32,128]{3,2,1,0:T(8,128)}), f32[16,2,32,128]{3,2,1,0:T(8,128)S(1)}, u32[]{:S(2)}, u32[]{:S(2)}) async-start(f32[16,2,32,128]{3,2,1,0:T(8,128)} %fusion), calls=%async_computation.3 | async-start | bytes 1048576 | tf_op jit(solution)/shard_map/all_to_all | solution.py:217

commit v3 on v2

--- a/solution.py
+++ b/solution.py
@@ -242,7 +242,7 @@
     planes = lax.axis_size("z")
     kv_shape = shape(PEERS, 2, ROWS, HEAD_DIM)
     q_shape = shape(PEERS, 4, ROWS, HEAD_DIM)
-    own = exchanged(call(pack_kv_kernel, kv_shape, (keys, values), cost=1))
+    own = exchanged(call(pack_kv_kernel, kv_shape, (keys, values), cost=1, vmem=60))
     packed = call(pack_q_kernel, q_shape, (queries, out_grad), cost=1)
     own, packed = lax.optimization_barrier((own, packed))
     rows = exchanged(packed)

time: 101 us -> 100 us (0.990)
  local copies, waits for them, and re-layouts: 1.94 us -> 0.04 us
    unnamed x8 -> x4, local copies, waits for them, and re-layouts: 1.9 us -> 0.01 us
    pallas_call x5, Pallas kernels: 15.5 us -> 16.5 us  [call(): pl.pallas_call(kernel, out_shape=outs, in_specs=[VMEM] * len(ins), out_sp...]
where the time goes in v3:
time: 100 us; the launch traced here: 99.5 us
  waiting for transfers between devices  48.4 us (48%)
  starting transfers between devices  32.5 us (32%)
  Pallas kernels  16.5 us (16%)
  other arithmetic  1.2 us (1%)
    all_to_all x4, waiting for transfers between devices, exchanged(): return lax.all_to_all(x, PLANE_AXES, 0, 0, tiled=True)  28.5 us
    all_to_all x4, starting transfers between devices, exchanged(): return lax.all_to_all(x, PLANE_AXES, 0, 0, tiled=True)  19.8 us
    pallas_call x5, Pallas kernels, call(): pl.pallas_call(kernel, out_shape=outs, in_specs=[VMEM] * len(ins), out_sp...  16.5 us
    ppermute x1, waiting for transfers between devices, per_device(): returned = lax.ppermute(ghalo, 'z', [(i + 1, i) for i in range(planes - 1)])  15.5 us
    ppermute x3, starting transfers between devices, swapped(): return lax.ppermute(x, 'core', [(0, 1), (1, 0)])  5.74 us
    ppermute x1, starting transfers between devices, per_device(): halo = lax.ppermute(own, 'z', [(i, i + 1) for i in range(planes - 1)])  5.02 us
    ppermute x1, waiting for transfers between devices, per_device(): halo = lax.ppermute(own, 'z', [(i, i + 1) for i in range(planes - 1)])  4.41 us
  transfers between devices with their start and end apart: 9, of which 6 were waited for; matrix products, arithmetic and copies ran while one was open for 1% of the time, Pallas kernels for 4%

profile of v3, /device:TPU:224, one launch (start us, length us, event | category | flops | bytes accessed | tf_op | source)
XLA Modules:
  0.0 99.5 jit_solution(2170660399464608203)
XLA Ops:
  0.6 2.1 %shard_map.75 = f32[16,2,32,128]{3,2,1,0:T(8,128)} custom-call(f32[32,16,128]{2,1,0:T(8,128)} %k_ref.1, f32[32,16,128]{2,1,0:T(8,128)} %v_ref.1), custom_call_target="tpu_custom_call" | custom-call | flops 1000000000 | bytes 3000000 | tf_op jit(solution)/shard_map/pallas_call | solution.py:205
  2.7 7.2 %all-to-all-start = ((f32[16,2,32,128]{3,2,1,0:T(8,128)}), f32[16,2,32,128]{3,2,1,0:T(8,128)S(1)}, u32[]{:S(2)}, u32[]{:S(2)}) async-start(f32[16,2,32,128]{3,2,1,0:T(8,128)} %shard_map.75), calls=%async_computation | async-start | bytes 1048576 | tf_op jit(solution)/shard_map/all_to_all | solution.py:217
  9.9 1.7 %shard_map.76 = f32[16,4,32,128]{3,2,1,0:T(8,128)} custom-call(f32[32,32,128]{2,1,0:T(8,128)S(1)} %copy-done, f32[32,32,128]{2,1,0:T(8,128)S(1)} %copy-done.1), custom_call_target="tpu_custom_call" | custom-call | flops 1000000000 | bytes 3000000 | tf_op jit(solution)/shard_map/pallas_call | solution.py:205
  11.6 9.9 %all-to-all-done.own_in = f32[16,2,32,128]{3,2,1,0:T(8,128)S(1)} async-done(((f32[16,2,32,128]{3,2,1,0:T(8,128)}), f32[16,2,32,128]{3,2,1,0:T(8,128)S(1)}, u32[]{:S(2)}, u32[]{:S(2)}) %all-to-all-start) | async-done | bytes 524320 | tf_op jit(solution)/shard_map/all_to_all | solution.py:217
  21.4 5.0 %collective-permute-start.1 = (f32[16,2,32,128]{3,2,1,0:T(8,128)S(1)}, f32[16,2,32,128]{3,2,1,0:T(8,128)S(1)}, u32[]{:S(2)}, u32[]{:S(2)}) collective-permute-start(f32[16,2,32,128]{3,2,1,0:T(8,128)S(1)} %all-to-all-done.own_in), channel_id=1, source_target_pairs={{0,32},{32,64},{64,96},{96,128},{128,160},{160,192},{192,224},{224... | collective-permute-start | bytes 1572872 | tf_op jit(solution)/shard_map/ppermute | solution.py:249
  26.5 3.7 %all-to-all-start.1 = ((f32[16,4,32,128]{3,2,1,0:T(8,128)}), f32[16,4,32,128]{3,2,1,0:T(8,128)S(1)}, u32[]{:S(2)}, u32[]{:S(2)}) async-start(f32[16,4,32,128]{3,2,1,0:T(8,128)} %shard_map.76), calls=%async_computation.1 | async-start | bytes 2097152 | tf_op jit(solution)/shard_map/all_to_all | solution.py:217
  30.1 1.9 %collective-permute-start = (f32[16,2,32,128]{3,2,1,0:T(8,128)S(1)}, f32[16,2,32,128]{3,2,1,0:T(8,128)S(1)}, u32[]{:S(2)}, u32[]{:S(2)}) collective-permute-start(f32[16,2,32,128]{3,2,1,0:T(8,128)S(1)} %all-to-all-done.own_in), channel_id=1, source_target_pairs={{0,8},{8,0},{1,9},{9,1},{2,10},{10,2},{3,11},{11,3},{4,12},{12,4},... | collective-permute-start | bytes 1572872 | tf_op jit(solution)/shard_map/ppermute | solution.py:221
  32.1 4.4 %collective-permute-done.1.halo_in = f32[16,2,32,128]{3,2,1,0:T(8,128)S(1)} collective-permute-done((f32[16,2,32,128]{3,2,1,0:T(8,128)S(1)}, f32[16,2,32,128]{3,2,1,0:T(8,128)S(1)}, u32[]{:S(2)}, u32[]{:S(2)}) %collective-permute-start.1) | collective-permute-done | bytes 524320 | tf_op jit(solution)/shard_map/ppermute | solution.py:249
  36.5 1.9 %collective-permute-start.2 = (f32[16,2,32,128]{3,2,1,0:T(8,128)S(1)}, f32[16,2,32,128]{3,2,1,0:T(8,128)S(1)}, u32[]{:S(2)}, u32[]{:S(2)}) collective-permute-start(f32[16,2,32,128]{3,2,1,0:T(8,128)S(1)} %collective-permute-done.1.halo_in), channel_id=1, source_target_pairs={{0,8},{8,0},{1,9},{9,1},{2,10},{10,2},{3,11},{11,3},{4,12},{12,4},... | collective-permute-start | bytes 1572872 | tf_op jit(solution)/shard_map/ppermute | solution.py:221
  38.4 0.0 collective-permute-done
  38.4 8.0 %all-to-all-done.1.rows_in = f32[16,4,32,128]{3,2,1,0:T(8,128)S(1)} async-done(((f32[16,4,32,128]{3,2,1,0:T(8,128)}), f32[16,4,32,128]{3,2,1,0:T(8,128)S(1)}, u32[]{:S(2)}, u32[]{:S(2)}) %all-to-all-start.1) | async-done | bytes 1048608 | tf_op jit(solution)/shard_map/all_to_all | solution.py:217
  46.5 0.2 maximum_select_fusion.other_in
  46.7 9.7 %shard_map.77 = (f32[16,4,32,128]{3,2,1,0:T(8,128)}, f32[32,2,32,128]{3,2,1,0:T(8,128)S(1)}, f32[32,2,32,128]{3,2,1,0:T(8,128)}) custom-call(f32[16,4,32,128]{3,2,1,0:T(8,128)S(1)} %all-to-all-done.1.rows_in, f32[16,2,32,128]{3,2,1,0:T(8,128)S(1)} %all-to-all-done.own_in, f32[16,2,32,128]{3,2,1,0:T(8,128)S(1)} %collective-permute-done.1.halo_in, ...), custom_call_target="tpu_custom_call" | custom-call | flops 8000000000 | bytes 24000000 | tf_op jit(solution)/shard_map/pallas_call | solution.py:205
  56.3 1.9 %collective-permute-start.3 = (f32[32,2,32,128]{3,2,1,0:T(8,128)}, f32[32,2,32,128]{3,2,1,0:T(8,128)S(1)}, u32[]{:S(2)}, u32[]{:S(2)}) collective-permute-start(f32[32,2,32,128]{3,2,1,0:T(8,128)} %get-tuple-element.25), channel_id=1, source_target_pairs={{0,8},{8,0},{1,9},{9,1},{2,10},{10,2},{3,11},{11,3},{4,12},{12,4},... | collective-permute-start | bytes 3145736 | tf_op jit(solution)/shard_map/ppermute | solution.py:221
  58.3 3.7 %all-to-all-start.2 = ((f32[16,4,32,128]{3,2,1,0:T(8,128)}), f32[16,4,32,128]{3,2,1,0:T(8,128)S(1)}, u32[]{:S(2)}, u32[]{:S(2)}) async-start(f32[16,4,32,128]{3,2,1,0:T(8,128)} %get-tuple-element.21), calls=%async_computation.2 | async-start | bytes 2097152 | tf_op jit(solution)/shard_map/all_to_all | solution.py:217
  61.9 0.1 slice_add_fusion
  62.0 1.9 %collective-permute-start.4 = (f32[16,2,32,128]{3,2,1,0:T(8,128)S(1)}, f32[16,2,32,128]{3,2,1,0:T(8,128)S(1)}, u32[]{:S(2)}, u32[]{:S(2)}) collective-permute-start(f32[16,2,32,128]{3,2,1,0:T(8,128)S(1)} %slice_add_fusion), channel_id=1, source_target_pairs={{32,0},{64,32},{96,64},{128,96},{160,128},{192,160},{224,192},{256... | collective-permute-start | bytes 1572872 | tf_op jit(solution)/shard_map/ppermute | solution.py:263
  64.0 15.5 %collective-permute-done.4 = f32[16,2,32,128]{3,2,1,0:T(8,128)S(1)} collective-permute-done((f32[16,2,32,128]{3,2,1,0:T(8,128)S(1)}, f32[16,2,32,128]{3,2,1,0:T(8,128)S(1)}, u32[]{:S(2)}, u32[]{:S(2)}) %collective-permute-start.4) | collective-permute-done | bytes 524320 | tf_op jit(solution)/shard_map/ppermute | solution.py:263
  79.5 1.0 fusion
  80.4 1.5 %all-to-all-done.2.in_ref = f32[16,4,32,128]{3,2,1,0:T(8,128)S(1)} async-done(((f32[16,4,32,128]{3,2,1,0:T(8,128)}), f32[16,4,32,128]{3,2,1,0:T(8,128)S(1)}, u32[]{:S(2)}, u32[]{:S(2)}) %all-to-all-start.2) | async-done | bytes 1048608 | tf_op jit(solution)/shard_map/all_to_all | solution.py:217
  82.0 5.3 %all-to-all-start.3 = ((f32[16,2,32,128]{3,2,1,0:T(8,128)}), f32[16,2,32,128]{3,2,1,0:T(8,128)S(1)}, u32[]{:S(2)}, u32[]{:S(2)}) async-start(f32[16,2,32,128]{3,2,1,0:T(8,128)} %fusion), calls=%async_computation.3 | async-start | bytes 1048576 | tf_op jit(solution)/shard_map/all_to_all | solution.py:217
  87.3 2.0 %shard_map.78 = (f32[32,32,128]{2,1,0:T(8,128)}, f32[32,32,128]{2,1,0:T(8,128)}) custom-call(f32[16,4,32,128]{3,2,1,0:T(8,128)S(1)} %all-to-all-done.2.in_ref), custom_call_target="tpu_custom_call" | custom-call | flops 1000000000 | bytes 3000000 | tf_op jit(solution)/shard_map/pallas_call | solution.py:205
  89.3 9.1 %all-to-all-done.3.in_ref = f32[16,2,32,128]{3,2,1,0:T(8,128)S(1)} async-done(((f32[16,2,32,128]{3,2,1,0:T(8,128)}), f32[16,2,32,128]{3,2,1,0:T(8,128)S(1)}, u32[]{:S(2)}, u32[]{:S(2)}) %all-to-all-start.3) | async-done | bytes 524320 | tf_op jit(solution)/shard_map/all_to_all | solution.py:217
  98.4 1.1 %shard_map.79 = (f32[32,16,128]{2,1,0:T(8,128)}, f32[32,16,128]{2,1,0:T(8,128)}) custom-call(f32[16,2,32,128]{3,2,1,0:T(8,128)S(1)} %all-to-all-done.3.in_ref), custom_call_target="tpu_custom_call" | custom-call | flops 1000000000 | bytes 3000000 | tf_op jit(solution)/shard_map/pallas_call | solution.py:205
  (8 shorter events, 0.0 us)
Async XLA Ops:
  2.7 7.2 %copy-start = (f32[32,32,128]{2,1,0:T(8,128)S(1)}, f32[32,32,128]{2,1,0:T(8,128)}, u32[]{:S(2)}) copy-start(f32[32,32,128]{2,1,0:T(8,128)} %q_ref.1) | copy-start | bytes 1572868
  2.7 7.2 %copy-start.1 = (f32[32,32,128]{2,1,0:T(8,128)S(1)}, f32[32,32,128]{2,1,0:T(8,128)}, u32[]{:S(2)}) copy-start(f32[32,32,128]{2,1,0:T(8,128)} %d_ref.1) | copy-start | bytes 1572868
  2.7 18.7 %all-to-all-start = ((f32[16,2,32,128]{3,2,1,0:T(8,128)}), f32[16,2,32,128]{3,2,1,0:T(8,128)S(1)}, u32[]{:S(2)}, u32[]{:S(2)}) async-start(f32[16,2,32,128]{3,2,1,0:T(8,128)} %shard_map.75), calls=%async_computation | async-start | bytes 1048576 | tf_op jit(solution)/shard_map/all_to_all | solution.py:217
  21.4 15.0 %collective-permute-start.1 = (f32[16,2,32,128]{3,2,1,0:T(8,128)S(1)}, f32[16,2,32,128]{3,2,1,0:T(8,128)S(1)}, u32[]{:S(2)}, u32[]{:S(2)}) collective-permute-start(f32[16,2,32,128]{3,2,1,0:T(8,128)S(1)} %all-to-all-done.own_in), channel_id=1, source_target_pairs={{0,32},{32,64},{64,96},{96,128},{128,160},{160,192},{192,224},{224... | collective-permute-start | bytes 1572872 | tf_op jit(solution)/shard_map/ppermute | solution.py:249
  26.5 20.0 %all-to-all-start.1 = ((f32[16,4,32,128]{3,2,1,0:T(8,128)}), f32[16,4,32,128]{3,2,1,0:T(8,128)S(1)}, u32[]{:S(2)}, u32[]{:S(2)}) async-start(f32[16,4,32,128]{3,2,1,0:T(8,128)} %shard_map.76), calls=%async_computation.1 | async-start | bytes 2097152 | tf_op jit(solution)/shard_map/all_to_all | solution.py:217
  30.1 8.3 %collective-permute-start = (f32[16,2,32,128]{3,2,1,0:T(8,128)S(1)}, f32[16,2,32,128]{3,2,1,0:T(8,128)S(1)}, u32[]{:S(2)}, u32[]{:S(2)}) collective-permute-start(f32[16,2,32,128]{3,2,1,0:T(8,128)S(1)} %all-to-all-done.own_in), channel_id=1, source_target_pairs={{0,8},{8,0},{1,9},{9,1},{2,10},{10,2},{3,11},{11,3},{4,12},{12,4},... | collective-permute-start | bytes 1572872 | tf_op jit(solution)/shard_map/ppermute | solution.py:221
  36.5 10.0 %collective-permute-start.2 = (f32[16,2,32,128]{3,2,1,0:T(8,128)S(1)}, f32[16,2,32,128]{3,2,1,0:T(8,128)S(1)}, u32[]{:S(2)}, u32[]{:S(2)}) collective-permute-start(f32[16,2,32,128]{3,2,1,0:T(8,128)S(1)} %collective-permute-done.1.halo_in), channel_id=1, source_target_pairs={{0,8},{8,0},{1,9},{9,1},{2,10},{10,2},{3,11},{11,3},{4,12},{12,4},... | collective-permute-start | bytes 1572872 | tf_op jit(solution)/shard_map/ppermute | solution.py:221
  56.3 5.6 %collective-permute-start.3 = (f32[32,2,32,128]{3,2,1,0:T(8,128)}, f32[32,2,32,128]{3,2,1,0:T(8,128)S(1)}, u32[]{:S(2)}, u32[]{:S(2)}) collective-permute-start(f32[32,2,32,128]{3,2,1,0:T(8,128)} %get-tuple-element.25), channel_id=1, source_target_pairs={{0,8},{8,0},{1,9},{9,1},{2,10},{10,2},{3,11},{11,3},{4,12},{12,4},... | collective-permute-start | bytes 3145736 | tf_op jit(solution)/shard_map/ppermute | solution.py:221
  58.3 23.7 %all-to-all-start.2 = ((f32[16,4,32,128]{3,2,1,0:T(8,128)}), f32[16,4,32,128]{3,2,1,0:T(8,128)S(1)}, u32[]{:S(2)}, u32[]{:S(2)}) async-start(f32[16,4,32,128]{3,2,1,0:T(8,128)} %get-tuple-element.21), calls=%async_computation.2 | async-start | bytes 2097152 | tf_op jit(solution)/shard_map/all_to_all | solution.py:217
  62.0 17.4 %collective-permute-start.4 = (f32[16,2,32,128]{3,2,1,0:T(8,128)S(1)}, f32[16,2,32,128]{3,2,1,0:T(8,128)S(1)}, u32[]{:S(2)}, u32[]{:S(2)}) collective-permute-start(f32[16,2,32,128]{3,2,1,0:T(8,128)S(1)} %slice_add_fusion), channel_id=1, source_target_pairs={{32,0},{64,32},{96,64},{128,96},{160,128},{192,160},{224,192},{256... | collective-permute-start | bytes 1572872 | tf_op jit(solution)/shard_map/ppermute | solution.py:263
  82.0 16.4 %all-to-all-start.3 = ((f32[16,2,32,128]{3,2,1,0:T(8,128)}), f32[16,2,32,128]{3,2,1,0:T(8,128)S(1)}, u32[]{:S(2)}, u32[]{:S(2)}) async-start(f32[16,2,32,128]{3,2,1,0:T(8,128)} %fusion), calls=%async_computation.3 | async-start | bytes 1048576 | tf_op jit(solution)/shard_map/all_to_all | solution.py:217

commit v4 on v3

--- a/solution.py
+++ b/solution.py
@@ -28,9 +28,22 @@
 
 
 def pack_kv_kernel(k_ref, v_ref, out_ref):
-    for g in range(GROUPS):
+    for g in range(GROUPS // 2):
         out_ref[g, 0] = k_ref[:, g, :]
         out_ref[g, 1] = v_ref[:, g, :]
+
+
+def pack_kv_call(keys, values):
+    half = GROUPS // 2
+    heads = pl.BlockSpec((ROWS, half, HEAD_DIM), lambda i: (0, i, 0))
+    return pl.pallas_call(
+        pack_kv_kernel,
+        out_shape=shape(PEERS, 2, ROWS, HEAD_DIM),
+        grid=(2,),
+        in_specs=[heads, heads],
+        out_specs=pl.BlockSpec((half, 2, ROWS, HEAD_DIM), lambda i: (i, 0, 0, 0)),
+        compiler_params=params(60),
+    )(keys, values)
 
 
 def pack_q_kernel(q_ref, d_ref, out_ref):
@@ -73,12 +86,12 @@
 ):
     z = lax.axis_index("z")
     core = lax.axis_index("core")
-    for r in range(7):
-        here = pl.ds(r * BLOCK, BLOCK)
-        for i, cat, tr in ((0, kcat, kt), (1, vcat, vt)):
+    def prepare(i, blocks):
+        cat, tr = ((kcat, kt), (vcat, vt))[i]
+        for r in blocks:
+            here = pl.ds(r * BLOCK, BLOCK)
             ref, at = (other_in, 8 * (r // 2)) if r % 2 else (halo_in if r < 4 else own_in, 8 * (r // 2 % 2))
-            x = ref[at : at + 8, i]
-            x = x.reshape(BLOCK, HEAD_DIM)
+            x = ref[at : at + 8, i].reshape(BLOCK, HEAD_DIM)
             hi, lo = split(x)
             cat[here, :HEAD_DIM] = hi
             cat[here, HEAD_DIM : 2 * HEAD_DIM] = lo
@@ -86,6 +99,7 @@
             thi, tlo = split(x.T)
             tr[:HEAD_DIM, here] = thi
             tr[HEAD_DIM:, here] = tlo
+
     key_iota = lax.broadcasted_iota(jnp.int32, (BLOCK, BLOCK), 0)
     query_iota = lax.broadcasted_iota(jnp.int32, (BLOCK, BLOCK), 1)
     later = key_iota > query_iota
@@ -113,6 +127,7 @@
             if b < 4:
                 m = jnp.where(exists(y, b), m, -jnp.inf)
             row_max = m if row_max is None else jnp.maximum(row_max, m)
+            yield
         qw_ref[y, h * BLOCK : (h + 1) * BLOCK, :] = jnp.concatenate([q_hi, q_lo], axis=1)
         state[y, h] = row_max
 
@@ -129,6 +144,7 @@
             s_ref[i, b] = w
             wcat[y, b * BLOCK : (b + 1) * BLOCK, h * 512 : h * 512 + 256] = hi
             wcat[y, b * BLOCK : (b + 1) * BLOCK, h * 512 + 256 : h * 512 + 512] = lo
+            yield
         vts = vt[:, 2 * y * BLOCK : 2 * y * BLOCK + SPAN]
         both = dot(vts, wcat[y, :, h * 512 : h * 512 + 256])
         at_sum = both[:HEAD_DIM] + both[HEAD_DIM:] + dot(vts[:HEAD_DIM], wcat[y, :, h * 512 + 256 : h * 512 + 512])
@@ -152,49 +168,56 @@
             hi, lo = split(s_ref[i, b] * (dp - row_dots))
             dscat[y, b * BLOCK : (b + 1) * BLOCK, h * 512 : h * 512 + 256] = hi
             dscat[y, b * BLOCK : (b + 1) * BLOCK, h * 512 + 256 : h * 512 + 512] = lo
+            yield
         kts = kt[:, 2 * y * BLOCK : 2 * y * BLOCK + SPAN]
         both = dot(kts, dscat[y, :, h * 512 : h * 512 + 256])
         dq = both[:HEAD_DIM] + both[HEAD_DIM:] + dot(kts[:HEAD_DIM], dscat[y, :, h * 512 + 256 : h * 512 + 512])
         dq = dq * query_scale
         out_buf[8 * y : 8 * y + 8, 2 + h] = dq.T.reshape(8, ROWS, HEAD_DIM)
 
-    def key_sums(y):
-        for kind, cat, weight_ref in ((0, dscat, qw_ref), (1, wcat, dw_ref)):
-            zero = jnp.zeros((BLOCK, HEAD_DIM), bf16)
-            parts = []
-            for h in range(2):
-                both = weight_ref[y, h * BLOCK : (h + 1) * BLOCK, :]
-                parts += [both, jnp.concatenate([both[:, :HEAD_DIM], zero], axis=1)]
-            weights = jnp.concatenate(parts, axis=0)
-            for b in range(5):
-                both = dot(cat[y, b * BLOCK : (b + 1) * BLOCK, :], weights)
-                part = both[:, :HEAD_DIM] + both[:, HEAD_DIM:]
-                if kind == 0:
-                    part = part * LN2
-                r = 2 * y + b
-                at = pl.ds(8 * (r // 2), 8) if r % 2 == 0 else pl.ds(pl.multiple_of(8 * (r // 2 + core), 8), 8)
-                ref = gmine if r % 2 == 0 else gother
-                part = part.reshape(8, ROWS, HEAD_DIM)
-                if y == 1 and b < 3:
-                    part = part + ref[at, kind]
-                ref[at, kind] = part
+    def key_sums(y, kind):
+        cat, weight_ref = ((dscat, qw_ref), (wcat, dw_ref))[kind]
+        zero = jnp.zeros((BLOCK, HEAD_DIM), bf16)
+        parts = []
+        for h in range(2):
+            both = weight_ref[y, h * BLOCK : (h + 1) * BLOCK, :]
+            parts += [both, jnp.concatenate([both[:, :HEAD_DIM], zero], axis=1)]
+        weights = jnp.concatenate(parts, axis=0)
+        for b in range(5):
+            both = dot(cat[y, b * BLOCK : (b + 1) * BLOCK, :], weights)
+            part = both[:, :HEAD_DIM] + both[:, HEAD_DIM:]
+            if kind == 0:
+                part = part * LN2
+            r = 2 * y + b
+            at = pl.ds(8 * (r // 2), 8) if r % 2 == 0 else pl.ds(pl.multiple_of(8 * (r // 2 + core), 8), 8)
+            ref = gmine if r % 2 == 0 else gother
+            part = part.reshape(8, ROWS, HEAD_DIM)
+            if y == 1 and b < 3:
+                part = part + ref[at, kind]
+            ref[at, kind] = part
+            yield
+
+    def run(*stages):
+        stages = list(stages)
+        while stages:
+            for stage in list(stages):
+                if next(stage, stage) is stage:
+                    stages.remove(stage)
 
     unused = pl.ds(pl.multiple_of(24 * (1 - core), 8), 8)
     gother[unused, :] = jnp.zeros((8, 2, ROWS, HEAD_DIM), f32)
-    scores(0, 0)
-    scores(0, 1)
-    weigh(0, 0)
-    scores(1, 0)
-    weigh(0, 1)
-    grads(0, 0)
-    scores(1, 1)
-    weigh(1, 0)
-    grads(0, 1)
-    key_sums(0)
-    weigh(1, 1)
-    grads(1, 0)
-    grads(1, 1)
-    key_sums(1)
+    prepare(0, range(7))
+    prepare(1, range(7))
+    run(scores(0, 0))
+    run(scores(0, 1))
+    run(weigh(0, 0), scores(1, 0))
+    run(weigh(0, 1), scores(1, 1))
+    run(grads(0, 0), weigh(1, 0))
+    run(grads(0, 1), weigh(1, 1))
+    run(grads(1, 0), key_sums(0, 1))
+    run(grads(1, 1), key_sums(0, 0))
+    run(key_sums(1, 1))
+    run(key_sums(1, 0))
 
 
 def shape(*dims):
@@ -242,7 +265,7 @@
     planes = lax.axis_size("z")
     kv_shape = shape(PEERS, 2, ROWS, HEAD_DIM)
     q_shape = shape(PEERS, 4, ROWS, HEAD_DIM)
-    own = exchanged(call(pack_kv_kernel, kv_shape, (keys, values), cost=1, vmem=60))
+    own = exchanged(pack_kv_call(keys, values))
     packed = call(pack_q_kernel, q_shape, (queries, out_grad), cost=1)
     own, packed = lax.optimization_barrier((own, packed))
     rows = exchanged(packed)

time: 100 us -> 100 us (level)
    pallas_call x5 -> x4, Pallas kernels: 16.5 us -> 14.4 us  [call(): pl.pallas_call(kernel, out_shape=outs, in_specs=[VMEM] * len(ins), out_sp...]
    pallas_call x0 -> x1, Pallas kernels: none -> 1.98 us  [pack_kv_call(): pl.pallas_call(pack_kv_kernel, out_shape=shape(PEERS, 2, ROWS, HEAD_DIM),...]
where the time goes in v4:
time: 100 us; the launch traced here: 99.3 us
  waiting for transfers between devices  48.4 us (48%)
  starting transfers between devices  32.5 us (32%)
  Pallas kernels  16.4 us (16%)
  other arithmetic  1.2 us (1%)
    all_to_all x4, waiting for transfers between devices, exchanged(): return lax.all_to_all(x, PLANE_AXES, 0, 0, tiled=True)  28.5 us
    all_to_all x4, starting transfers between devices, exchanged(): return lax.all_to_all(x, PLANE_AXES, 0, 0, tiled=True)  19.8 us
    ppermute x1, waiting for transfers between devices, per_device(): returned = lax.ppermute(ghalo, 'z', [(i + 1, i) for i in range(planes - 1)])  15.5 us
    pallas_call x4, Pallas kernels, call(): pl.pallas_call(kernel, out_shape=outs, in_specs=[VMEM] * len(ins), out_sp...  14.4 us
    ppermute x3, starting transfers between devices, swapped(): return lax.ppermute(x, 'core', [(0, 1), (1, 0)])  5.74 us
    ppermute x1, starting transfers between devices, per_device(): halo = lax.ppermute(own, 'z', [(i, i + 1) for i in range(planes - 1)])  5.02 us
    ppermute x1, waiting for transfers between devices, per_device(): halo = lax.ppermute(own, 'z', [(i, i + 1) for i in range(planes - 1)])  4.41 us
  transfers between devices with their start and end apart: 9, of which 6 were waited for; matrix products, arithmetic and copies ran while one was open for 1% of the time, Pallas kernels for 4%

profile of v4, /device:TPU:224, one launch (start us, length us, event | category | flops | bytes accessed | tf_op | source)
XLA Modules:
  0.0 99.3 jit_solution(11745881839370272487)
XLA Ops:
  0.6 2.0 %shard_map.75 = f32[16,2,32,128]{3,2,1,0:T(8,128)} custom-call(f32[32,16,128]{2,1,0:T(8,128)} %k_ref.1, f32[32,16,128]{2,1,0:T(8,128)} %v_ref.1), custom_call_target="tpu_custom_call" | custom-call | tf_op jit(solution)/shard_map/pallas_call | solution.py:39
  2.6 7.2 %all-to-all-start = ((f32[16,2,32,128]{3,2,1,0:T(8,128)}), f32[16,2,32,128]{3,2,1,0:T(8,128)S(1)}, u32[]{:S(2)}, u32[]{:S(2)}) async-start(f32[16,2,32,128]{3,2,1,0:T(8,128)} %shard_map.75), calls=%async_computation | async-start | bytes 1048576 | tf_op jit(solution)/shard_map/all_to_all | solution.py:240
  9.8 1.7 %shard_map.76 = f32[16,4,32,128]{3,2,1,0:T(8,128)} custom-call(f32[32,32,128]{2,1,0:T(8,128)S(1)} %copy-done, f32[32,32,128]{2,1,0:T(8,128)S(1)} %copy-done.1), custom_call_target="tpu_custom_call" | custom-call | flops 1000000000 | bytes 3000000 | tf_op jit(solution)/shard_map/pallas_call | solution.py:228
  11.5 9.9 %all-to-all-done.own_in = f32[16,2,32,128]{3,2,1,0:T(8,128)S(1)} async-done(((f32[16,2,32,128]{3,2,1,0:T(8,128)}), f32[16,2,32,128]{3,2,1,0:T(8,128)S(1)}, u32[]{:S(2)}, u32[]{:S(2)}) %all-to-all-start) | async-done | bytes 524320 | tf_op jit(solution)/shard_map/all_to_all | solution.py:240
  21.3 5.0 %collective-permute-start.1 = (f32[16,2,32,128]{3,2,1,0:T(8,128)S(1)}, f32[16,2,32,128]{3,2,1,0:T(8,128)S(1)}, u32[]{:S(2)}, u32[]{:S(2)}) collective-permute-start(f32[16,2,32,128]{3,2,1,0:T(8,128)S(1)} %all-to-all-done.own_in), channel_id=1, source_target_pairs={{0,32},{32,64},{64,96},{96,128},{128,160},{160,192},{192,224},{224... | collective-permute-start | bytes 1572872 | tf_op jit(solution)/shard_map/ppermute | solution.py:272
  26.4 3.7 %all-to-all-start.1 = ((f32[16,4,32,128]{3,2,1,0:T(8,128)}), f32[16,4,32,128]{3,2,1,0:T(8,128)S(1)}, u32[]{:S(2)}, u32[]{:S(2)}) async-start(f32[16,4,32,128]{3,2,1,0:T(8,128)} %shard_map.76), calls=%async_computation.1 | async-start | bytes 2097152 | tf_op jit(solution)/shard_map/all_to_all | solution.py:240
  30.0 1.9 %collective-permute-start = (f32[16,2,32,128]{3,2,1,0:T(8,128)S(1)}, f32[16,2,32,128]{3,2,1,0:T(8,128)S(1)}, u32[]{:S(2)}, u32[]{:S(2)}) collective-permute-start(f32[16,2,32,128]{3,2,1,0:T(8,128)S(1)} %all-to-all-done.own_in), channel_id=1, source_target_pairs={{0,8},{8,0},{1,9},{9,1},{2,10},{10,2},{3,11},{11,3},{4,12},{12,4},... | collective-permute-start | bytes 1572872 | tf_op jit(solution)/shard_map/ppermute | solution.py:244
  32.0 4.4 %collective-permute-done.1.halo_in = f32[16,2,32,128]{3,2,1,0:T(8,128)S(1)} collective-permute-done((f32[16,2,32,128]{3,2,1,0:T(8,128)S(1)}, f32[16,2,32,128]{3,2,1,0:T(8,128)S(1)}, u32[]{:S(2)}, u32[]{:S(2)}) %collective-permute-start.1) | collective-permute-done | bytes 524320 | tf_op jit(solution)/shard_map/ppermute | solution.py:272
  36.4 1.9 %collective-permute-start.2 = (f32[16,2,32,128]{3,2,1,0:T(8,128)S(1)}, f32[16,2,32,128]{3,2,1,0:T(8,128)S(1)}, u32[]{:S(2)}, u32[]{:S(2)}) collective-permute-start(f32[16,2,32,128]{3,2,1,0:T(8,128)S(1)} %collective-permute-done.1.halo_in), channel_id=1, source_target_pairs={{0,8},{8,0},{1,9},{9,1},{2,10},{10,2},{3,11},{11,3},{4,12},{12,4},... | collective-permute-start | bytes 1572872 | tf_op jit(solution)/shard_map/ppermute | solution.py:244
  38.3 0.0 collective-permute-done
  38.3 8.0 %all-to-all-done.1.rows_in = f32[16,4,32,128]{3,2,1,0:T(8,128)S(1)} async-done(((f32[16,4,32,128]{3,2,1,0:T(8,128)}), f32[16,4,32,128]{3,2,1,0:T(8,128)S(1)}, u32[]{:S(2)}, u32[]{:S(2)}) %all-to-all-start.1) | async-done | bytes 1048608 | tf_op jit(solution)/shard_map/all_to_all | solution.py:240
  46.4 0.2 maximum_select_fusion.other_in
  46.5 9.7 %shard_map.77 = (f32[16,4,32,128]{3,2,1,0:T(8,128)}, f32[32,2,32,128]{3,2,1,0:T(8,128)S(1)}, f32[32,2,32,128]{3,2,1,0:T(8,128)}) custom-call(f32[16,4,32,128]{3,2,1,0:T(8,128)S(1)} %all-to-all-done.1.rows_in, f32[16,2,32,128]{3,2,1,0:T(8,128)S(1)} %all-to-all-done.own_in, f32[16,2,32,128]{3,2,1,0:T(8,128)S(1)} %collective-permute-done.1.halo_in, ...), custom_call_target="tpu_custom_call" | custom-call | flops 8000000000 | bytes 24000000 | tf_op jit(solution)/shard_map/pallas_call | solution.py:228
  56.2 1.9 %collective-permute-start.3 = (f32[32,2,32,128]{3,2,1,0:T(8,128)}, f32[32,2,32,128]{3,2,1,0:T(8,128)S(1)}, u32[]{:S(2)}, u32[]{:S(2)}) collective-permute-start(f32[32,2,32,128]{3,2,1,0:T(8,128)} %get-tuple-element.25), channel_id=1, source_target_pairs={{0,8},{8,0},{1,9},{9,1},{2,10},{10,2},{3,11},{11,3},{4,12},{12,4},... | collective-permute-start | bytes 3145736 | tf_op jit(solution)/shard_map/ppermute | solution.py:244
  58.1 3.7 %all-to-all-start.2 = ((f32[16,4,32,128]{3,2,1,0:T(8,128)}), f32[16,4,32,128]{3,2,1,0:T(8,128)S(1)}, u32[]{:S(2)}, u32[]{:S(2)}) async-start(f32[16,4,32,128]{3,2,1,0:T(8,128)} %get-tuple-element.21), calls=%async_computation.2 | async-start | bytes 2097152 | tf_op jit(solution)/shard_map/all_to_all | solution.py:240
  61.8 0.1 slice_add_fusion
  61.9 1.9 %collective-permute-start.4 = (f32[16,2,32,128]{3,2,1,0:T(8,128)S(1)}, f32[16,2,32,128]{3,2,1,0:T(8,128)S(1)}, u32[]{:S(2)}, u32[]{:S(2)}) collective-permute-start(f32[16,2,32,128]{3,2,1,0:T(8,128)S(1)} %slice_add_fusion), channel_id=1, source_target_pairs={{32,0},{64,32},{96,64},{128,96},{160,128},{192,160},{224,192},{256... | collective-permute-start | bytes 1572872 | tf_op jit(solution)/shard_map/ppermute | solution.py:286
  63.8 15.5 %collective-permute-done.4 = f32[16,2,32,128]{3,2,1,0:T(8,128)S(1)} collective-permute-done((f32[16,2,32,128]{3,2,1,0:T(8,128)S(1)}, f32[16,2,32,128]{3,2,1,0:T(8,128)S(1)}, u32[]{:S(2)}, u32[]{:S(2)}) %collective-permute-start.4) | collective-permute-done | bytes 524320 | tf_op jit(solution)/shard_map/ppermute | solution.py:286
  79.3 1.0 fusion
  80.3 1.5 %all-to-all-done.2.in_ref = f32[16,4,32,128]{3,2,1,0:T(8,128)S(1)} async-done(((f32[16,4,32,128]{3,2,1,0:T(8,128)}), f32[16,4,32,128]{3,2,1,0:T(8,128)S(1)}, u32[]{:S(2)}, u32[]{:S(2)}) %all-to-all-start.2) | async-done | bytes 1048608 | tf_op jit(solution)/shard_map/all_to_all | solution.py:240
  81.8 5.3 %all-to-all-start.3 = ((f32[16,2,32,128]{3,2,1,0:T(8,128)}), f32[16,2,32,128]{3,2,1,0:T(8,128)S(1)}, u32[]{:S(2)}, u32[]{:S(2)}) async-start(f32[16,2,32,128]{3,2,1,0:T(8,128)} %fusion), calls=%async_computation.3 | async-start | bytes 1048576 | tf_op jit(solution)/shard_map/all_to_all | solution.py:240
  87.1 2.0 %shard_map.78 = (f32[32,32,128]{2,1,0:T(8,128)}, f32[32,32,128]{2,1,0:T(8,128)}) custom-call(f32[16,4,32,128]{3,2,1,0:T(8,128)S(1)} %all-to-all-done.2.in_ref), custom_call_target="tpu_custom_call" | custom-call | flops 1000000000 | bytes 3000000 | tf_op jit(solution)/shard_map/pallas_call | solution.py:228
  89.1 9.1 %all-to-all-done.3.in_ref = f32[16,2,32,128]{3,2,1,0:T(8,128)S(1)} async-done(((f32[16,2,32,128]{3,2,1,0:T(8,128)}), f32[16,2,32,128]{3,2,1,0:T(8,128)S(1)}, u32[]{:S(2)}, u32[]{:S(2)}) %all-to-all-start.3) | async-done | bytes 524320 | tf_op jit(solution)/shard_map/all_to_all | solution.py:240
  98.2 1.1 %shard_map.79 = (f32[32,16,128]{2,1,0:T(8,128)}, f32[32,16,128]{2,1,0:T(8,128)}) custom-call(f32[16,2,32,128]{3,2,1,0:T(8,128)S(1)} %all-to-all-done.3.in_ref), custom_call_target="tpu_custom_call" | custom-call | flops 1000000000 | bytes 3000000 | tf_op jit(solution)/shard_map/pallas_call | solution.py:228
  (8 shorter events, 0.0 us)
Async XLA Ops:
  2.6 7.2 %copy-start = (f32[32,32,128]{2,1,0:T(8,128)S(1)}, f32[32,32,128]{2,1,0:T(8,128)}, u32[]{:S(2)}) copy-start(f32[32,32,128]{2,1,0:T(8,128)} %q_ref.1) | copy-start | bytes 1572868
  2.6 7.2 %copy-start.1 = (f32[32,32,128]{2,1,0:T(8,128)S(1)}, f32[32,32,128]{2,1,0:T(8,128)}, u32[]{:S(2)}) copy-start(f32[32,32,128]{2,1,0:T(8,128)} %d_ref.1) | copy-start | bytes 1572868
  2.6 18.7 %all-to-all-start = ((f32[16,2,32,128]{3,2,1,0:T(8,128)}), f32[16,2,32,128]{3,2,1,0:T(8,128)S(1)}, u32[]{:S(2)}, u32[]{:S(2)}) async-start(f32[16,2,32,128]{3,2,1,0:T(8,128)} %shard_map.75), calls=%async_computation | async-start | bytes 1048576 | tf_op jit(solution)/shard_map/all_to_all | solution.py:240
  21.3 15.0 %collective-permute-start.1 = (f32[16,2,32,128]{3,2,1,0:T(8,128)S(1)}, f32[16,2,32,128]{3,2,1,0:T(8,128)S(1)}, u32[]{:S(2)}, u32[]{:S(2)}) collective-permute-start(f32[16,2,32,128]{3,2,1,0:T(8,128)S(1)} %all-to-all-done.own_in), channel_id=1, source_target_pairs={{0,32},{32,64},{64,96},{96,128},{128,160},{160,192},{192,224},{224... | collective-permute-start | bytes 1572872 | tf_op jit(solution)/shard_map/ppermute | solution.py:272
  26.4 20.0 %all-to-all-start.1 = ((f32[16,4,32,128]{3,2,1,0:T(8,128)}), f32[16,4,32,128]{3,2,1,0:T(8,128)S(1)}, u32[]{:S(2)}, u32[]{:S(2)}) async-start(f32[16,4,32,128]{3,2,1,0:T(8,128)} %shard_map.76), calls=%async_computation.1 | async-start | bytes 2097152 | tf_op jit(solution)/shard_map/all_to_all | solution.py:240
  30.0 8.3 %collective-permute-start = (f32[16,2,32,128]{3,2,1,0:T(8,128)S(1)}, f32[16,2,32,128]{3,2,1,0:T(8,128)S(1)}, u32[]{:S(2)}, u32[]{:S(2)}) collective-permute-start(f32[16,2,32,128]{3,2,1,0:T(8,128)S(1)} %all-to-all-done.own_in), channel_id=1, source_target_pairs={{0,8},{8,0},{1,9},{9,1},{2,10},{10,2},{3,11},{11,3},{4,12},{12,4},... | collective-permute-start | bytes 1572872 | tf_op jit(solution)/shard_map/ppermute | solution.py:244
  36.4 10.0 %collective-permute-start.2 = (f32[16,2,32,128]{3,2,1,0:T(8,128)S(1)}, f32[16,2,32,128]{3,2,1,0:T(8,128)S(1)}, u32[]{:S(2)}, u32[]{:S(2)}) collective-permute-start(f32[16,2,32,128]{3,2,1,0:T(8,128)S(1)} %collective-permute-done.1.halo_in), channel_id=1, source_target_pairs={{0,8},{8,0},{1,9},{9,1},{2,10},{10,2},{3,11},{11,3},{4,12},{12,4},... | collective-permute-start | bytes 1572872 | tf_op jit(solution)/shard_map/ppermute | solution.py:244
  56.2 5.6 %collective-permute-start.3 = (f32[32,2,32,128]{3,2,1,0:T(8,128)}, f32[32,2,32,128]{3,2,1,0:T(8,128)S(1)}, u32[]{:S(2)}, u32[]{:S(2)}) collective-permute-start(f32[32,2,32,128]{3,2,1,0:T(8,128)} %get-tuple-element.25), channel_id=1, source_target_pairs={{0,8},{8,0},{1,9},{9,1},{2,10},{10,2},{3,11},{11,3},{4,12},{12,4},... | collective-permute-start | bytes 3145736 | tf_op jit(solution)/shard_map/ppermute | solution.py:244
  58.1 23.7 %all-to-all-start.2 = ((f32[16,4,32,128]{3,2,1,0:T(8,128)}), f32[16,4,32,128]{3,2,1,0:T(8,128)S(1)}, u32[]{:S(2)}, u32[]{:S(2)}) async-start(f32[16,4,32,128]{3,2,1,0:T(8,128)} %get-tuple-element.21), calls=%async_computation.2 | async-start | bytes 2097152 | tf_op jit(solution)/shard_map/all_to_all | solution.py:240
  61.9 17.4 %collective-permute-start.4 = (f32[16,2,32,128]{3,2,1,0:T(8,128)S(1)}, f32[16,2,32,128]{3,2,1,0:T(8,128)S(1)}, u32[]{:S(2)}, u32[]{:S(2)}) collective-permute-start(f32[16,2,32,128]{3,2,1,0:T(8,128)S(1)} %slice_add_fusion), channel_id=1, source_target_pairs={{32,0},{64,32},{96,64},{128,96},{160,128},{192,160},{224,192},{256... | collective-permute-start | bytes 1572872 | tf_op jit(solution)/shard_map/ppermute | solution.py:286
  81.8 16.4 %all-to-all-start.3 = ((f32[16,2,32,128]{3,2,1,0:T(8,128)}), f32[16,2,32,128]{3,2,1,0:T(8,128)S(1)}, u32[]{:S(2)}, u32[]{:S(2)}) async-start(f32[16,2,32,128]{3,2,1,0:T(8,128)} %fusion), calls=%async_computation.3 | async-start | bytes 1048576 | tf_op jit(solution)/shard_map/all_to_all | solution.py:240
